TPU v7x, 512 devices: a whole 4x8x8 slice. The times are simulated.
512 devices in a mesh: dp: 4 (over y_lo, core), expert: 32 (over y_hi, z), seq: 4 (over x).
Axes of the slice: x: 4, y: 8 (y_hi: 4, y_lo: 2; y = y_hi * 2 + y_lo), z: 8, core: 2. Of those that a mesh axis runs over, the one named last changes fastest.
Arguments:
- codes: bfloat16 [65536, 2048], P(('dp', 'expert', 'seq')), may hold values from -6 to 6
- scales: float32 [65536, 16], P(('dp', 'expert', 'seq')), may hold values from 0.3 to 3
- grad_out: bfloat16 [65536, 2048], P(('dp', 'expert', 'seq')), may hold values from -6 to 6
- route_weight: float32 [65536, 2], P(('dp', 'expert', 'seq')), may hold values from 0.2 to 1
- expert_ids: int32 [65536, 2], P(('dp', 'expert', 'seq')), may hold values from 0 to 127, all different within a row; in each aligned block of 128 rows (0 to 127, 128 to 255, ...) at most 4 rows name the same one
- w_gate: bfloat16 [128, 2048, 384], P(('expert', 'seq'), 'dp'), may hold values from -0.125 to 0.125
- w_up: bfloat16 [128, 2048, 384], P(('expert', 'seq'), 'dp'), may hold values from -0.125 to 0.125
- w_down: bfloat16 [128, 384, 2048], P(('expert', 'seq'), None, 'dp'), may hold values from -0.3125 to 0.3125
Outputs:
- grad_input: bfloat16 [65536, 2048], P(('dp', 'expert', 'seq'))
- grad_gate: bfloat16 [128, 2048, 384], P(('expert', 'seq'), 'dp')
- grad_up: bfloat16 [128, 2048, 384], P(('expert', 'seq'), 'dp')
- grad_down: bfloat16 [128, 384, 2048], P(('expert', 'seq'))
Inputs may be any that keep to these rules, and one draw needn't show every extreme that they name: `expert_ids`: each token names 2 different experts. Among the 128 tokens of one device no expert is named more than 4 times, and in every draw some expert is named exactly 4 times by the tokens of some device.
All inputs are finite; a program needn't handle non-finite values.
Results may differ from a plain program's by a relative error of at most 0.013.
Values may be sent and summed in bfloat16 or wider, within the bound.
No kernel may reach another device: no remote copies, remote signals or barrier semaphores. Data moves between devices by JAX's collectives and lax.ppermute only.
A program may use at most 64 MiB of HBM per device.

v0:
```python
import jax
import jax.numpy as jnp
from jax import lax
from jax.sharding import PartitionSpec as P


def slot_table(routed, experts, capacity):
    flat = routed.reshape(-1)
    onehot = (flat[:, None] == jnp.arange(experts, dtype=jnp.int32)[None, :]).astype(jnp.int32)
    before = jnp.cumsum(onehot, axis=0) - onehot
    rank = jnp.sum(before * onehot, axis=1)
    return flat * capacity + rank


def expert_backward(rows_x, rows_dy, gate_mat, up_mat, down_mat):
    pre_gate = jnp.dot(rows_x, gate_mat, preferred_element_type=jnp.float32)
    pre_up = jnp.dot(rows_x, up_mat, preferred_element_type=jnp.float32)
    gate_sig = jax.nn.sigmoid(pre_gate)
    gate_act = pre_gate * gate_sig
    hidden = (gate_act * pre_up).astype(jnp.bfloat16)
    d_hidden = lax.dot_general(
        rows_dy, down_mat, (((1,), (1,)), ((), ())), preferred_element_type=jnp.float32
    )
    d_gate = (d_hidden * pre_up * gate_sig * (1.0 + pre_gate * (1.0 - gate_sig))).astype(
        jnp.bfloat16
    )
    d_up = (d_hidden * gate_act).astype(jnp.bfloat16)
    grad_d = lax.dot_general(
        hidden, rows_dy, (((0,), (0,)), ((), ())), preferred_element_type=jnp.float32
    )
    grad_g = lax.dot_general(
        rows_x, d_gate, (((0,), (0,)), ((), ())), preferred_element_type=jnp.float32
    )
    grad_u = lax.dot_general(
        rows_x, d_up, (((0,), (0,)), ((), ())), preferred_element_type=jnp.float32
    )
    back = lax.dot_general(
        d_gate, gate_mat, (((1,), (1,)), ((), ())), preferred_element_type=jnp.float32
    )
    back = back + lax.dot_general(
        d_up, up_mat, (((1,), (1,)), ((), ())), preferred_element_type=jnp.float32
    )
    return (back.astype(jnp.bfloat16), grad_g, grad_u, grad_d)


def per_device(codes, scales, grad_out, route_weight, expert_ids, w_gate, w_up, w_down):
    tok_rows, features = codes.shape
    top_k = expert_ids.shape[1]
    assigned = tok_rows * top_k
    outer = lax.axis_size("expert")
    inner = lax.axis_size("seq")
    groups = outer * inner
    capacity = 2 * assigned // groups
    slot_count = groups * capacity
    inputs = (
        (codes.astype(jnp.float32).reshape(tok_rows, features // 128, 128) * scales[:, :, None])
        .reshape(tok_rows, features)
        .astype(jnp.bfloat16)
    )
    scaled = (
        (route_weight[:, :, None] * grad_out.astype(jnp.float32)[:, None, :])
        .astype(jnp.bfloat16)
        .reshape(assigned, features)
    )
    position = slot_table(expert_ids, groups, capacity)
    owners = (
        jnp.full((slot_count,), assigned, jnp.int32)
        .at[position]
        .set(jnp.arange(assigned, dtype=jnp.int32))
    )
    filled = (owners < assigned)[:, None]
    token_of = jnp.minimum(owners, assigned - 1)
    zero_rows = jnp.zeros((), jnp.bfloat16)
    x_send = jnp.where(filled, inputs[token_of // top_k], zero_rows).reshape(
        groups, capacity, features
    )
    dy_send = jnp.where(filled, scaled[token_of], zero_rows).reshape(groups, capacity, features)
    x_recv, dy_recv = (
        lax.all_to_all(x_send, ("expert", "seq"), split_axis=0, concat_axis=0, tiled=True),
        lax.all_to_all(dy_send, ("expert", "seq"), split_axis=0, concat_axis=0, tiled=True),
    )
    gate_full, up_full, down_full = (
        lax.all_gather(w_gate, "dp", axis=1, tiled=True),
        lax.all_gather(w_up, "dp", axis=1, tiled=True),
        lax.all_gather(w_down, "dp", axis=2, tiled=True),
    )
    back, grad_g, grad_u, grad_d = expert_backward(
        x_recv.reshape(slot_count, features),
        dy_recv.reshape(slot_count, features),
        gate_full[0],
        up_full[0],
        down_full[0],
    )
    back_recv = lax.all_to_all(
        back.reshape(groups, capacity, features),
        ("expert", "seq"),
        split_axis=0,
        concat_axis=0,
        tiled=True,
    )
    picked = back_recv.reshape(slot_count, features)[position].reshape(tok_rows, top_k, features)
    grad_input = jnp.sum(picked.astype(jnp.float32), axis=1).astype(jnp.bfloat16)
    summed_gate, summed_up = (
        lax.psum_scatter(
            grad_g[None].astype(jnp.bfloat16), "dp", scatter_dimension=1, tiled=True
        ).astype(jnp.float32),
        lax.psum_scatter(
            grad_u[None].astype(jnp.bfloat16), "dp", scatter_dimension=1, tiled=True
        ).astype(jnp.float32),
    )
    summed_down = lax.psum(grad_d[None].astype(jnp.bfloat16), "dp")
    return (
        grad_input,
        summed_gate.astype(jnp.bfloat16),
        summed_up.astype(jnp.bfloat16),
        summed_down,
    )


def solution(mesh):
    placed = (
        P(("dp", "expert", "seq"), None),
        P(("dp", "expert", "seq"), None),
        P(("dp", "expert", "seq"), None),
        P(("dp", "expert", "seq"), None),
        P(("dp", "expert", "seq"), None),
        P(("expert", "seq"), "dp", None),
        P(("expert", "seq"), "dp", None),
        P(("expert", "seq"), None, "dp"),
    )
    return jax.shard_map(
        per_device,
        mesh=mesh,
        in_specs=placed,
        out_specs=(
            P(("dp", "expert", "seq"), None),
            P(("expert", "seq"), "dp", None),
            P(("expert", "seq"), "dp", None),
            P(("expert", "seq"), None, None),
        ),
        check_vma=False,
    )
```

profile of v0, /device:TPU:1, one launch (start us, length us, event | category | flops | bytes accessed | tf_op | source)
XLA Modules:
  0.0 383.4 jit_solution(11709933348253569552)
XLA Ops:
  14.0 2.5 gather_fusion.1
  19.7 2.5 mul.76
  24.0 2.5 gather_fusion
  26.4 2.2 gather.14
  28.7 5.0 %broadcast_select_fusion.1 = (bf16[128,4,2048]{2,1,0:T(4,128)(2,1)}, bf16[128,4,2048]{2,1,0:T(4,128)(2,1)}) fusion(bf16[128,4,2048]{2,1,0:T(4,128)(2,1)} %gather.14, pred[128,4]{1,0:T(8,128)(4,1)S(1)} %broadcast_in_dim.34, bf16[128,4,2048]{2,1,0:T(4,128)(2,1)} %gather.16), kind=kLoop, calls=%fused_computation.13 | loop fusion | flops 2097152 | bytes 8389120 | tf_op jit(solution)/shard_map/jit(_where)/select_n | solution.py:77
  33.7 20.8 %all-to-all-start = ((bf16[128,4,2048]{2,1,0:T(4,128)(2,1)}), bf16[128,4,2048]{2,1,0:T(4,128)(2,1)S(1)}, u32[]{:S(2)}, u32[]{:S(2)}) async-start(bf16[128,4,2048]{2,1,0:T(4,128)(2,1)} %get-tuple-element.6), calls=%async_computation | async-start | bytes 4194304 | tf_op jit(solution)/shard_map/all_to_all | solution.py:80
  55.3 64.2 %all-to-all-done = bf16[128,4,2048]{2,1,0:T(4,128)(2,1)S(1)} async-done(((bf16[128,4,2048]{2,1,0:T(4,128)(2,1)}), bf16[128,4,2048]{2,1,0:T(4,128)(2,1)S(1)}, u32[]{:S(2)}, u32[]{:S(2)}) %all-to-all-start) | async-done | bytes 2097184 | tf_op jit(solution)/shard_map/all_to_all | solution.py:80
  119.5 7.8 %all-to-all-start.1 = ((bf16[128,4,2048]{2,1,0:T(4,128)(2,1)}), bf16[128,4,2048]{2,1,0:T(4,128)(2,1)}, u32[]{:S(2)}, u32[]{:S(2)}) async-start(bf16[128,4,2048]{2,1,0:T(4,128)(2,1)} %get-tuple-element.7), calls=%async_computation.1 | async-start | bytes 4194304 | tf_op jit(solution)/shard_map/all_to_all | solution.py:79
  131.1 59.6 %all-to-all-done.1 = bf16[128,4,2048]{2,1,0:T(4,128)(2,1)} async-done(((bf16[128,4,2048]{2,1,0:T(4,128)(2,1)}), bf16[128,4,2048]{2,1,0:T(4,128)(2,1)}, u32[]{:S(2)}, u32[]{:S(2)}) %all-to-all-start.1) | async-done | bytes 2097184 | tf_op jit(solution)/shard_map/all_to_all | solution.py:79
  190.7 2.5 reshape.98
  193.3 3.4 fusion.5
  196.7 3.0 fusion.8
  200.7 2.3 fusion.2
  203.0 15.4 %all-gather.4.cloned.1.call-done = bf16[1,384,2048]{2,1,0:T(8,128)(2,1)} async-done(((bf16[1,384,512]{2,1,0:T(8,128)(2,1)}), bf16[1,384,2048]{2,1,0:T(8,128)(2,1)}) %all-gather.4.cloned.1.call-update) | async-done | bytes 1572880 | tf_op jit(solution)/shard_map/all_gather | solution.py:85
  218.4 3.9 %multiply_convert_fusion.2 = (bf16[512,384]{1,0:T(8,128)(2,1)S(1)}, bf16[512,384]{1,0:T(8,128)(2,1)S(1)}) fusion(f32[512,384]{1,0:T(8,128)} %copy-done.7, f32[512,384]{1,0:T(8,128)} %copy-done.8, bf16[512,2048]{1,0:T(8,128)(2,1)} %reshape.97, bf16[1,384,2048]{2,1,0:T(8,128)(2,1)} %all-gather.4.cloned.1.call-done), kind=kOutput, calls=%fused_computation.26 | convolution fusion | flops 807862272 | bytes 6029312 | tf_op jit(solution)/shard_map/dot_general | solution.py:21
  222.3 2.4 fusion
  231.1 16.4 %all-to-all-start.2 = ((bf16[128,4,2048]{2,1,0:T(4,128)(2,1)}), bf16[128,4,2048]{2,1,0:T(4,128)(2,1)}, u32[]{:S(2)}, u32[]{:S(2)}) async-start(bf16[128,4,2048]{2,1,0:T(4,128)(2,1)} %reshape.99), calls=%async_computation.2 | async-start | bytes 4194304 | tf_op jit(solution)/shard_map/all_to_all | solution.py:94
  247.8 2.5 fusion.1
  250.3 64.0 %all-to-all-done.2 = bf16[128,4,2048]{2,1,0:T(4,128)(2,1)} async-done(((bf16[128,4,2048]{2,1,0:T(4,128)(2,1)}), bf16[128,4,2048]{2,1,0:T(4,128)(2,1)}, u32[]{:S(2)}, u32[]{:S(2)}) %all-to-all-start.2) | async-done | bytes 2097184 | tf_op jit(solution)/shard_map/all_to_all | solution.py:94
  314.3 2.5 reshape.100
  318.9 3.6 reduce_sum.25
  322.5 18.3 %reduce-scatter.3.cloned.1.call-done = bf16[1,512,384]{2,1,0:T(8,128)(2,1)} async-done(((bf16[1,2048,384]{2,1,0:T(8,128)(2,1)}), bf16[1,512,384]{2,1,0:T(8,128)(2,1)}) %reduce-scatter.3.cloned.1.call-update) | async-done | bytes 393232 | tf_op jit(solution)/shard_map/reduce_scatter | solution.py:104
  340.8 33.0 %reduce-scatter.5.cloned.1.call-done = bf16[1,512,384]{2,1,0:T(8,128)(2,1)} async-done(((bf16[1,2048,384]{2,1,0:T(8,128)(2,1)}), bf16[1,512,384]{2,1,0:T(8,128)(2,1)}) %reduce-scatter.5.cloned.1.call-update) | async-done | bytes 393232 | tf_op jit(solution)/shard_map/reduce_scatter | solution.py:107
  373.8 2.7 copy.23
  (70 shorter events, 25.9 us)
Async XLA Ops:
  7.2 6.3 %copy-start.6 = (bf16[128,2048]{1,0:T(8,128)(2,1)S(1)}, bf16[128,2048]{1,0:T(8,128)(2,1)}, u32[]{:S(2)}) copy-start(bf16[128,2048]{1,0:T(8,128)(2,1)} %param.8) | copy-start | bytes 1572868
  16.4 2.2 copy-start.5
  33.7 85.8 %all-to-all-start = ((bf16[128,4,2048]{2,1,0:T(4,128)(2,1)}), bf16[128,4,2048]{2,1,0:T(4,128)(2,1)S(1)}, u32[]{:S(2)}, u32[]{:S(2)}) async-start(bf16[128,4,2048]{2,1,0:T(4,128)(2,1)} %get-tuple-element.6), calls=%async_computation | async-start | bytes 4194304 | tf_op jit(solution)/shard_map/all_to_all | solution.py:80
  54.5 138.7 %all-gather.8.cloned.1.call-start = ((), (), s32[]{:S(2)}) async-start(), calls=%async_computation.7 | async-start | bytes 1966080 | tf_op jit(solution)/shard_map/all_gather | solution.py:83
  119.5 71.2 %all-to-all-start.1 = ((bf16[128,4,2048]{2,1,0:T(4,128)(2,1)}), bf16[128,4,2048]{2,1,0:T(4,128)(2,1)}, u32[]{:S(2)}, u32[]{:S(2)}) async-start(bf16[128,4,2048]{2,1,0:T(4,128)(2,1)} %get-tuple-element.7), calls=%async_computation.1 | async-start | bytes 4194304 | tf_op jit(solution)/shard_map/all_to_all | solution.py:79
  127.3 69.4 %all-gather.6.cloned.1.call-start = ((), (), s32[]{:S(2)}) async-start(), calls=%async_computation.6 | async-start | bytes 1966080 | tf_op jit(solution)/shard_map/all_gather | solution.py:84
  128.1 90.3 %all-gather.4.cloned.1.call-start = ((), (), s32[]{:S(2)}) async-start(), calls=%async_computation.5 | async-start | bytes 1966080 | tf_op jit(solution)/shard_map/all_gather | solution.py:85
  128.8 193.7 %all-reduce.2.cloned.1.call-start = ((), (), s32[]{:S(2)}) async-start(), calls=%async_computation.10 | async-start | bytes 3145728 | tf_op jit(solution)/shard_map/psum | solution.py:111
  193.2 29.0 %copy-start = (bf16[512,2048]{1,0:T(8,128)(2,1)}, bf16[512,2048]{1,0:T(8,128)(2,1)S(1)}, u32[]{:S(2)}) copy-start(bf16[512,2048]{1,0:T(8,128)(2,1)S(1)} %reshape.98) | copy-start | bytes 6291460
  196.7 3.0 copy-start.7
  196.7 3.9 %copy-start.2 = (bf16[512,2048]{1,0:T(8,128)(2,1)S(1)}, bf16[512,2048]{1,0:T(8,128)(2,1)}, u32[]{:S(2)}) copy-start(bf16[512,2048]{1,0:T(8,128)(2,1)} %reshape.97) | copy-start | bytes 6291460
  199.7 1.0 copy-start.8
  203.0 137.8 %reduce-scatter.3.cloned.1.call-start = ((), (), s32[]{:S(2)}) async-start(), calls=%async_computation.8 | async-start | bytes 1966080 | tf_op jit(solution)/shard_map/reduce_scatter | solution.py:104
  224.7 1.4 copy-start.3
  226.1 1.4 copy-start.4
  231.1 16.7 %copy-start.1 = (bf16[512,2048]{1,0:T(8,128)(2,1)S(1)}, bf16[512,2048]{1,0:T(8,128)(2,1)}, u32[]{:S(2)}) copy-start(bf16[512,2048]{1,0:T(8,128)(2,1)} %copy-done) | copy-start | bytes 6291460
  231.1 83.2 %all-to-all-start.2 = ((bf16[128,4,2048]{2,1,0:T(4,128)(2,1)}), bf16[128,4,2048]{2,1,0:T(4,128)(2,1)}, u32[]{:S(2)}, u32[]{:S(2)}) async-start(bf16[128,4,2048]{2,1,0:T(4,128)(2,1)} %reshape.99), calls=%async_computation.2 | async-start | bytes 4194304 | tf_op jit(solution)/shard_map/all_to_all | solution.py:94
  247.5 126.3 %reduce-scatter.5.cloned.1.call-start = ((), (), s32[]{:S(2)}) async-start(), calls=%async_computation.9 | async-start | bytes 1966080 | tf_op jit(solution)/shard_map/reduce_scatter | solution.py:107
Sparse Core Ops, SparseCore 0:
  57.5 55.7 all-gather.7
  130.3 52.8 all-gather.5
  185.3 33.0 all-gather.3
  221.2 86.6 all-reduce.1
  311.1 29.6 reduce-scatter.2
  344.1 29.6 reduce-scatter.4
where the time goes:
time: 384 us; the launch traced here: 383 us
  waiting for transfers between devices  257 us (67%)
  starting transfers between devices  45.7 us (12%)
  local copies, waits for them, and re-layouts  34.6 us (9%)
  matrix products  20 us (5%)
  between operations  14.4 us (4%)
  other arithmetic  12.1 us (3%)
    all_to_all x1, waiting for transfers between devices, per_device(): lax.all_to_all(dy_send, ('expert', 'seq'), split_axis=0, concat_axis=0, t...  64.2 us
    all_to_all x1, waiting for transfers between devices, per_device(): lax.all_to_all(back.reshape(groups, capacity, features), ('expert', 'seq'...  64 us
    all_to_all x1, waiting for transfers between devices, per_device(): lax.all_to_all(x_send, ('expert', 'seq'), split_axis=0, concat_axis=0, ti...  59.6 us
    reduce_scatter x1, waiting for transfers between devices, per_device(): lax.psum_scatter(grad_u[None].astype(jnp.bfloat16), 'dp', scatter_dimensi...  33 us
    all_to_all x1, starting transfers between devices, per_device(): lax.all_to_all(dy_send, ('expert', 'seq'), split_axis=0, concat_axis=0, t...  20.8 us
    reduce_scatter x1, waiting for transfers between devices, per_device(): lax.psum_scatter(grad_g[None].astype(jnp.bfloat16), 'dp', scatter_dimensi...  18.3 us
    all_to_all x1, starting transfers between devices, per_device(): lax.all_to_all(back.reshape(groups, capacity, features), ('expert', 'seq'...  16.4 us
    all_gather x1, waiting for transfers between devices, per_device(): lax.all_gather(w_down, 'dp', axis=2, tiled=True)  15.4 us
  transfers between devices with their start and end apart: 9, of which 6 were waited for; matrix products, arithmetic and copies ran while one was open for 9% of the time, Pallas kernels for 0%

commit v1 on v0

v1 whole, which is shorter than its diff:
```python
import functools

import jax
import jax.numpy as jnp
from jax import lax
from jax.experimental import pallas as pl
from jax.experimental.pallas import tpu as pltpu
from jax.sharding import PartitionSpec as P

BF16 = jnp.bfloat16
F32 = jnp.float32
I32 = jnp.int32

OTHER_CORE = [(0, 1), (1, 0), (2, 3), (3, 2)]
OTHER_CHIP = [(0, 2), (2, 0), (1, 3), (3, 1)]


def iota(shape, dim):
    return lax.broadcasted_iota(I32, shape, dim)


def as_bf16(mask):
    return jnp.where(mask, 1.0, 0.0).astype(BF16)


def vmem(*_):
    return pl.BlockSpec(memory_space=pltpu.VMEM)


def send_kernel(experts, cap, dp_ref, ids_ref, weight_ref, scale_ref, codes_ref, grad_ref, send_ref, row_ref, table, place):
    step = pl.program_id(0)
    tokens, features = codes_ref.shape
    width = features // 4
    rows = send_ref.shape[0]

    @pl.when(step == 0)
    def _():
        ids = ids_ref[...]
        expert = iota((experts, tokens), 0)
        first, second = expert == ids[0:1, :], expert == ids[1:2, :]
        earlier = as_bf16(iota((tokens, tokens), 0) < iota((tokens, tokens), 1))
        count = jnp.dot(as_bf16(first | second), earlier, preferred_element_type=F32)
        rank0 = jnp.sum(jnp.where(first, count, 0.0), axis=0, keepdims=True)
        rank1 = jnp.sum(jnp.where(second, count, 0.0), axis=0, keepdims=True)
        row0 = 2 * cap * ids[0:1, :] + rank0.astype(I32)
        row1 = 2 * cap * ids[1:2, :] + rank1.astype(I32)
        place[0:1, :] = row0
        place[1:2, :] = row1
        both = jnp.concatenate([row0.astype(F32), row1.astype(F32), jnp.zeros((tokens - 2, tokens), F32)], axis=0)
        row_ref[...] = both.T.astype(I32)
        blocks = scale_ref.shape[0]
        scale = jnp.concatenate([scale_ref[...], jnp.zeros((tokens - blocks, tokens), F32)], axis=0).T
        lanes = features // blocks
        for j in range(blocks):
            part = slice(j * lanes, (j + 1) * lanes)
            table[0:tokens, part] = (codes_ref[:, part].astype(F32) * scale[:, j : j + 1]).astype(BF16)
        table[tokens : 2 * tokens, :] = grad_ref[...]

    row = iota((rows, tokens), 0) + step * rows
    is_grad = (row & cap) != 0
    base = row - (row & cap)
    in0, in1 = base == place[0:1, :], base == place[1:2, :]
    weight = jnp.sum(
        jnp.where(in0, weight_ref[0:1, :], 0.0) + jnp.where(in1, weight_ref[1:2, :], 0.0), axis=1, keepdims=True
    )
    weight = jnp.where(is_grad[:, 0:1], weight, 1.0)
    inside = in0 | in1
    pick = jnp.concatenate([as_bf16(inside & jnp.logical_not(is_grad)), as_bf16(inside & is_grad)], axis=1)
    for r in range(4):
        start = pl.multiple_of((dp_ref[0] ^ r) * width, width)
        rows_r = jnp.dot(pick, table[:, pl.ds(start, width)], preferred_element_type=F32)
        send_ref[:, r * width : (r + 1) * width] = (rows_r * weight).astype(BF16)


def rows_to_send(dp, ids, weights, scales, codes, grads, experts, cap):
    tokens, features = codes.shape
    total = 2 * experts * cap
    rows = 256
    whole = lambda a: pl.BlockSpec(a.shape, lambda i: (0, 0))
    return pl.pallas_call(
        functools.partial(send_kernel, experts, cap),
        grid=(total // rows,),
        in_specs=[pl.BlockSpec(memory_space=pltpu.SMEM)] + [whole(a) for a in (ids, weights, scales, codes, grads)],
        out_specs=[pl.BlockSpec((rows, features), lambda i: (i, 0)), pl.BlockSpec((tokens, tokens), lambda i: (0, 0))],
        out_shape=[
            jax.ShapeDtypeStruct((total, features), BF16),
            jax.ShapeDtypeStruct((tokens, tokens), I32),
        ],
        scratch_shapes=[pltpu.VMEM((2 * tokens, features), BF16), pltpu.VMEM((8, tokens), I32)],
        compiler_params=pltpu.CompilerParams(vmem_limit_bytes=32 << 20),
        cost_estimate=pl.CostEstimate(flops=2 * total * 2 * tokens * features, bytes_accessed=6 << 20, transcendentals=0),
    )(dp, ids, weights, scales, codes, grads)


def gather_matrix(cap, rows):
    q, j = iota((rows, rows), 0), iota((rows, rows), 1)
    half = rows // 2
    slot = q & (half - 1)
    row = (slot >> 2) * (2 * cap) + (slot & (cap - 1))
    return as_bf16(j == jnp.where(q >= half, row + cap, row))


def spread_matrix(cap, rows):
    q, j = iota((rows, rows), 1), iota((rows, rows), 0)
    half = rows // 2
    slot = q & (half - 1)
    row = (slot >> 2) * (2 * cap) + (slot & (cap - 1))
    return as_bf16(j == jnp.where(q >= half, row + cap, row))


def expert_kernel(cap, *refs):
    recv = refs[0]
    gate, up, down = refs[1:5], refs[5:9], refs[9:13]
    back, x_even, x_odd, dy_even, dy_odd, d_gate, d_up, hidden = refs[13:21]
    pre_g, pre_u, d_hid = refs[21:24]
    slots = d_gate.shape[0]
    width = x_even.shape[2]
    block = 256
    half = block // 2
    xs = [x_even.at[0], x_odd.at[0], x_even.at[1], x_odd.at[1]]
    dys = [dy_even.at[0], dy_odd.at[0], dy_even.at[1], dy_odd.at[1]]

    gather = gather_matrix(cap, block)
    for b in range(2 * slots // block):
        for r in range(4):
            part = jnp.dot(
                gather,
                recv[b * block : (b + 1) * block, r * width : (r + 1) * width],
                preferred_element_type=F32,
            ).astype(BF16)
            xs[r][b * half : (b + 1) * half, :] = part[:half]
            dys[r][b * half : (b + 1) * half, :] = part[half:]

    def total(rows, mats, dims):
        acc = None
        for r in range(4):
            term = lax.dot_general(rows[r][...], mats[r][...], dims, preferred_element_type=F32)
            acc = term if acc is None else acc + term
        return acc

    plain = (((1,), (0,)), ((), ()))
    turned = (((1,), (1,)), ((), ()))
    pre_g[...] = total(xs, gate, plain)
    pre_u[...] = total(xs, up, plain)
    d_hid[...] = total(dys, down, turned)

    step = 64

    @pl.loop(0, slots // step)
    def _(i):
        at = pl.ds(pl.multiple_of(i * step, step), step)
        pg, pu, dh = pre_g[at, :], pre_u[at, :], d_hid[at, :]
        sig = jax.nn.sigmoid(pg)
        act = pg * sig
        hidden[at, :] = (act * pu).astype(BF16)
        d_gate[at, :] = (dh * pu * sig * (1.0 + pg * (1.0 - sig))).astype(BF16)
        d_up[at, :] = (dh * act).astype(BF16)

    spread = spread_matrix(cap, block)
    for r in range(2):
        halves = []
        for p in range(2):
            value = lax.dot_general(d_gate[...], gate[2 * p + r][...], turned, preferred_element_type=F32)
            value = value + lax.dot_general(d_up[...], up[2 * p + r][...], turned, preferred_element_type=F32)
            halves.append(value.astype(BF16))
        for b in range(2 * slots // block):
            at = slice(b * half, (b + 1) * half)
            rows = jnp.concatenate([halves[0][at], halves[1][at]], axis=0)
            back[b * block : (b + 1) * block, r * width : (r + 1) * width] = jnp.dot(
                spread, rows, preferred_element_type=F32
            ).astype(BF16)


def expert_rows(recv, gate, up, down, cap):
    total, features = recv.shape
    slots = total // 2
    width = features // 4
    hid = gate[0].shape[1]
    shape = jax.ShapeDtypeStruct
    return pl.pallas_call(
        functools.partial(expert_kernel, cap),
        in_specs=[vmem()] * 13,
        out_specs=[vmem()] * 8,
        out_shape=[shape((total, features // 2), BF16)]
        + [shape((2, slots, width), BF16)] * 4
        + [shape((slots, hid), BF16)] * 3,
        scratch_shapes=[pltpu.VMEM((slots, hid), F32)] * 3,
        compiler_params=pltpu.CompilerParams(vmem_limit_bytes=48 << 20),
        cost_estimate=pl.CostEstimate(
            flops=2 * slots * features * hid * 5, bytes_accessed=16 << 20, transcendentals=slots * hid
        ),
    )(recv, *gate, *up, *down)


def token_kernel(cap, dp_ref, row_ref, recv_ref, out_ref):
    tokens, features = out_ref.shape
    width = features // 4
    total = recv_ref.shape[0]
    row0, row1 = row_ref[:, 0:1], row_ref[:, 1:2]
    at = iota((tokens, total), 1)
    low = as_bf16((at == row0) | (at == row1))
    high = as_bf16((at == row0 + cap) | (at == row1 + cap))
    for p, pick in enumerate((low, high)):
        for r in range(2):
            value = jnp.dot(pick, recv_ref[:, r * width : (r + 1) * width], preferred_element_type=F32)
            start = pl.multiple_of((dp_ref[0] ^ (2 * p + r)) * width, width)
            out_ref[:, pl.ds(start, width)] = value.astype(BF16)


def token_rows(dp, row_of, recv, tokens, features, cap):
    return pl.pallas_call(
        functools.partial(token_kernel, cap),
        in_specs=[pl.BlockSpec(memory_space=pltpu.SMEM), vmem(), vmem()],
        out_specs=vmem(),
        out_shape=jax.ShapeDtypeStruct((tokens, features), BF16),
        compiler_params=pltpu.CompilerParams(vmem_limit_bytes=32 << 20),
        cost_estimate=pl.CostEstimate(flops=4 * tokens * features * recv.shape[0], bytes_accessed=3 << 20, transcendentals=0),
    )(dp, row_of, recv)


def gathered(own):
    chip = lax.ppermute(own, "dp", OTHER_CHIP)
    return [own, lax.ppermute(own, "dp", OTHER_CORE), chip, lax.ppermute(chip, "dp", OTHER_CORE)]


def partial_sum(blocks, grads):
    return lax.dot_general(blocks, grads, (((1,), (0,)), ((), ())), preferred_element_type=F32).astype(BF16)


def add(a, b):
    return a.astype(F32) + b.astype(F32)


def scattered(even, odd, grads):
    given = lax.ppermute(partial_sum(odd, grads), "dp", OTHER_CORE)
    kept = add(partial_sum(even, grads), given)
    other = lax.ppermute(kept[1].astype(BF16), "dp", OTHER_CHIP)
    return add(kept[0], other).astype(BF16)


def place_kernel(dp_ref, even_ref, odd_ref, out_ref):
    width = even_ref.shape[2]
    for r, ref in enumerate((even_ref, odd_ref, even_ref, odd_ref)):
        start = pl.multiple_of((dp_ref[0] ^ r) * width, width)
        out_ref[:, pl.ds(start, width)] = ref[r // 2]


def summed(even, odd, hidden, dp):
    def product(dy):
        return jnp.stack(
            [
                lax.dot_general(hidden, dy[i], (((0,), (0,)), ((), ())), preferred_element_type=F32).astype(BF16)
                for i in range(2)
            ]
        )

    given = lax.ppermute(product(odd), "dp", OTHER_CORE)
    kept = add(product(even), given).astype(BF16)
    other = lax.ppermute(kept, "dp", OTHER_CHIP)
    mine = add(kept, other[::-1]).astype(BF16)
    theirs = lax.ppermute(mine, "dp", OTHER_CORE)
    hid, width = mine.shape[1:]
    return pl.pallas_call(
        place_kernel,
        in_specs=[pl.BlockSpec(memory_space=pltpu.SMEM), vmem(), vmem()],
        out_specs=vmem(),
        out_shape=jax.ShapeDtypeStruct((hid, 4 * width), BF16),
        compiler_params=pltpu.CompilerParams(vmem_limit_bytes=32 << 20),
        cost_estimate=pl.CostEstimate(flops=0, bytes_accessed=3 << 20, transcendentals=0),
    )(dp, mine, theirs)


def exchange(rows, groups):
    chunks = rows.reshape(groups, rows.shape[0] // groups, rows.shape[1])
    return lax.all_to_all(chunks, ("expert", "seq"), split_axis=0, concat_axis=0, tiled=True).reshape(rows.shape)


def per_device(codes, scales, grad_out, route_weight, expert_ids, w_gate, w_up, w_down):
    tokens, features = codes.shape
    groups = lax.axis_size("expert") * lax.axis_size("seq")
    cap = 2 * tokens * expert_ids.shape[1] // groups
    dp = lax.axis_index("dp").astype(I32).reshape(1)
    gate, up, down = gathered(w_gate[0]), gathered(w_up[0]), gathered(w_down[0])
    send, row_of = rows_to_send(dp, expert_ids.T, route_weight.T, scales.T, codes, grad_out, groups, cap)
    recv = exchange(send, groups)
    back, x_even, x_odd, dy_even, dy_odd, d_gate, d_up, hidden = expert_rows(recv, gate, up, down, cap)
    returned = exchange(back, groups)
    grad_gate = scattered(x_even, x_odd, d_gate)
    grad_up = scattered(x_even, x_odd, d_up)
    grad_down = summed(dy_even, dy_odd, hidden, dp)
    grad_input = token_rows(dp, row_of, returned, tokens, features, cap)
    return grad_input, grad_gate[None], grad_up[None], grad_down[None]


def solution(mesh):
    rows = P(("dp", "expert", "seq"), None)
    split = P(("expert", "seq"), "dp", None)
    return jax.shard_map(
        per_device,
        mesh=mesh,
        in_specs=(rows, rows, rows, rows, rows, split, split, P(("expert", "seq"), None, "dp")),
        out_specs=(rows, split, split, P(("expert", "seq"), None, None)),
        check_vma=False,
    )
```

time: 384 us -> 279 us (0.73)
  waiting for transfers between devices: 257 us -> 148 us
  starting transfers between devices: 45.7 us -> 88.3 us
  local copies, waits for them, and re-layouts: 34.6 us -> 14.8 us
  Pallas kernels: 0 us -> 17.5 us
  matrix products: 20 us -> 4.55 us
  between operations: 14.4 us -> 1.11 us
  other arithmetic: 12.1 us -> 2.59 us
    all_to_all x3 -> x2, waiting for transfers between devices: 188 us -> 0.01 us  [exchange(): lax.all_to_all(chunks, ('expert', 'seq'), split_axis=0, concat_axis=0, ti...]
    ppermute x0 -> x16, waiting for transfers between devices: none -> 148 us  [the longest x3 90.4 us: gathered(): chip = lax.ppermute(own, 'dp', OTHER_CHIP)]
    reduce_scatter x2 -> x0, waiting for transfers between devices: 51.3 us -> none  [the longest x1 33 us: per_device(): lax.psum_scatter(grad_u[None].astype(jnp.bfloat16), 'dp', scatter_dimensi...]
    ppermute x0 -> x16, starting transfers between devices: none -> 46.1 us  [the longest x3 10 us: gathered(): lax.ppermute(own, 'dp', OTHER_CORE)]
    pallas_call x0 -> x4, Pallas kernels: none -> 17.5 us  [the longest x1 12.2 us: expert_rows(): pl.pallas_call(functools.partial(expert_kernel, cap), in_specs=[vmem()] *...]
    dot_general x8, matrix products: 20 us -> 4.55 us  [the longest x4 2.97 us: partial_sum(): lax.dot_general(blocks, grads, (((1,), (0,)), ((), ())), preferred_elemen...]
    all_gather x3 -> x0, waiting for transfers between devices: 15.4 us -> none  [the longest x1 15.4 us: per_device(): lax.all_gather(w_down, 'dp', axis=2, tiled=True)]
    gather x5 -> x0, local copies, waits for them, and re-layouts: 10.8 us -> none  [the longest x2 4.71 us: per_device(): scaled[token_of]]
  transfers between devices with their start and end apart: 9 -> 18, of which waited for: 6 -> 6; matrix products, arithmetic and copies ran while one was open for 9% -> 3% of each run, Pallas kernels for 0% -> 0%
where the time goes in v1:
time: 279 us; the launch traced here: 277 us
  waiting for transfers between devices  148 us (53%)
  starting transfers between devices  88.3 us (32%)
  Pallas kernels  17.5 us (6%)
  local copies, waits for them, and re-layouts  14.8 us (5%)
  matrix products  4.55 us (2%)
    ppermute x3, waiting for transfers between devices, gathered(): chip = lax.ppermute(own, 'dp', OTHER_CHIP)  90.4 us
    ppermute x1, waiting for transfers between devices, summed(): other = lax.ppermute(kept, 'dp', OTHER_CHIP)  47.4 us
    all_to_all x2, starting transfers between devices, exchange(): lax.all_to_all(chunks, ('expert', 'seq'), split_axis=0, concat_axis=0, ti...  42.2 us
    unnamed x54, local copies, waits for them, and re-layouts  14.7 us
    pallas_call x1, Pallas kernels, expert_rows(): pl.pallas_call(functools.partial(expert_kernel, cap), in_specs=[vmem()] *...  12.2 us
    ppermute x3, starting transfers between devices, gathered(): lax.ppermute(own, 'dp', OTHER_CORE)  10 us
    ppermute x2, waiting for transfers between devices, scattered(): other = lax.ppermute(kept[1].astype(BF16), 'dp', OTHER_CHIP)  9.98 us
    ppermute x3, starting transfers between devices, gathered(): lax.ppermute(chip, 'dp', OTHER_CORE)  9.79 us
  transfers between devices with their start and end apart: 18, of which 6 were waited for; matrix products, arithmetic and copies ran while one was open for 3% of the time, Pallas kernels for 0%

profile of v1, /device:TPU:1, one launch (start us, length us, event | category | flops | bytes accessed | tf_op | source)
XLA Modules:
  0.0 276.7 jit_solution(13151156769812679565)
XLA Ops:
  4.8 2.5 shard_map.111
  7.3 2.0 copy-done
  9.9 21.5 %all-to-all-start = ((bf16[128,8,2048]{2,1,0:T(8,128)(2,1)}), bf16[128,8,2048]{2,1,0:T(8,128)(2,1)}, u32[]{:S(2)}, u32[]{:S(2)}) async-start(bf16[128,8,2048]{2,1,0:T(8,128)(2,1)} %bitcast.74), calls=%async_computation | async-start | bytes 8388608 | tf_op jit(solution)/shard_map/all_to_all | solution.py:275
  31.4 2.3 collective-permute-start.1
  33.8 3.1 %collective-permute-start = (bf16[512,384]{1,0:T(8,128)(2,1)S(1)}, bf16[512,384]{1,0:T(8,128)(2,1)S(1)}, u32[]{:S(2)}, u32[]{:S(2)}) collective-permute-start(bf16[512,384]{1,0:T(8,128)(2,1)S(1)} %bitcast.77), channel_id=1, source_target_pairs={{0,128},{128,0},{256,384},{384,256},{1,129},{129,1},{257,385},{385... | collective-permute-start | bytes 1179656 | tf_op jit(solution)/shard_map/ppermute | solution.py:223
  36.9 3.0 %collective-permute-start.4 = (bf16[512,384]{1,0:T(8,128)(2,1)S(1)}, bf16[512,384]{1,0:T(8,128)(2,1)S(1)}, u32[]{:S(2)}, u32[]{:S(2)}) collective-permute-start(bf16[512,384]{1,0:T(8,128)(2,1)S(1)} %bitcast.79), channel_id=1, source_target_pairs={{0,256},{256,0},{128,384},{384,128},{1,257},{257,1},{129,385},{385... | collective-permute-start | bytes 1179656 | tf_op jit(solution)/shard_map/ppermute | solution.py:222
  39.9 2.3 collective-permute-start.7
  42.2 2.5 collective-permute-start.3
  44.7 84.4 %collective-permute-done.1.refs_3_ = bf16[512,384]{1,0:T(8,128)(2,1)S(1)} collective-permute-done((bf16[512,384]{1,0:T(8,128)(2,1)S(1)}, bf16[512,384]{1,0:T(8,128)(2,1)S(1)}, u32[]{:S(2)}, u32[]{:S(2)}) %collective-permute-start.1) | collective-permute-done | bytes 393248 | tf_op jit(solution)/shard_map/ppermute | solution.py:222
  129.1 4.4 %collective-permute-start.6 = (bf16[384,512]{1,0:T(8,128)(2,1)S(1)}, bf16[384,512]{1,0:T(8,128)(2,1)S(1)}, u32[]{:S(2)}, u32[]{:S(2)}) collective-permute-start(bf16[384,512]{1,0:T(8,128)(2,1)S(1)} %bitcast.83), channel_id=1, source_target_pairs={{0,128},{128,0},{256,384},{384,256},{1,129},{129,1},{257,385},{385... | collective-permute-start | bytes 1179656 | tf_op jit(solution)/shard_map/ppermute | solution.py:223
  135.5 2.0 collective-permute-done.4.refs_7_
  137.5 4.5 %collective-permute-start.5 = (bf16[512,384]{1,0:T(8,128)(2,1)S(1)}, bf16[512,384]{1,0:T(8,128)(2,1)S(1)}, u32[]{:S(2)}, u32[]{:S(2)}) collective-permute-start(bf16[512,384]{1,0:T(8,128)(2,1)S(1)} %collective-permute-done.4.refs_7_), channel_id=1, source_target_pairs={{0,128},{128,0},{256,384},{384,256},{1,129},{129,1},{257,385},{385... | collective-permute-start | bytes 1179656 | tf_op jit(solution)/shard_map/ppermute | solution.py:223
  141.9 3.9 %collective-permute-done.7.refs_11_ = bf16[384,512]{1,0:T(8,128)(2,1)S(1)} collective-permute-done((bf16[384,512]{1,0:T(8,128)(2,1)S(1)}, bf16[384,512]{1,0:T(8,128)(2,1)S(1)}, u32[]{:S(2)}, u32[]{:S(2)}) %collective-permute-start.7) | collective-permute-done | bytes 393248 | tf_op jit(solution)/shard_map/ppermute | solution.py:222
  145.9 3.4 %collective-permute-start.8 = (bf16[384,512]{1,0:T(8,128)(2,1)S(1)}, bf16[384,512]{1,0:T(8,128)(2,1)S(1)}, u32[]{:S(2)}, u32[]{:S(2)}) collective-permute-start(bf16[384,512]{1,0:T(8,128)(2,1)S(1)} %collective-permute-done.7.refs_11_), channel_id=1, source_target_pairs={{0,128},{128,0},{256,384},{384,256},{1,129},{129,1},{257,385},{385... | collective-permute-start | bytes 1179656 | tf_op jit(solution)/shard_map/ppermute | solution.py:223
  154.6 12.2 %shard_map.112 = (bf16[1024,1024]{1,0:T(8,128)(2,1)}, bf16[2,512,512]{2,1,0:T(8,128)(2,1)}, bf16[2,512,512]{2,1,0:T(8,128)(2,1)}, bf16[2,512,512]{2,1,0:T(8,128)...) custom-call(bf16[1024,2048]{1,0:T(8,128)(2,1)} %bitcast.5.refs_0_, ...), custom_call_target="tpu_custom_call" | custom-call | flops 4026531840 | bytes 16777216 | tf_op jit(solution)/shard_map/pallas_call | solution.py:180
  169.0 20.7 %all-to-all-start.1 = ((bf16[128,8,1024]{2,1,0:T(8,128)(2,1)}), bf16[128,8,1024]{2,1,0:T(8,128)(2,1)S(1)}, u32[]{:S(2)}, u32[]{:S(2)}) async-start(bf16[128,8,1024]{2,1,0:T(8,128)(2,1)} %bitcast.88), calls=%async_computation.1 | async-start | bytes 4194304 | tf_op jit(solution)/shard_map/all_to_all | solution.py:275
  190.6 2.7 collective-permute-start.13
  197.7 2.4 collective-permute-start.9
  202.2 4.1 %collective-permute-start.14 = (bf16[2,384,512]{2,1,0:T(8,128)(2,1)S(1)}, bf16[2,384,512]{2,1,0:T(8,128)(2,1)S(1)}, u32[]{:S(2)}, u32[]{:S(2)}) collective-permute-start(bf16[2,384,512]{2,1,0:T(8,128)(2,1)S(1)} %add_convert_fusion.1), channel_id=1, source_target_pairs={{0,256},{256,0},{128,384},{384,128},{1,257},{257,1},{129,385},{385... | collective-permute-start | bytes 2359304 | tf_op jit(solution)/shard_map/ppermute | solution.py:259
  208.7 47.4 %collective-permute-done.14 = bf16[2,384,512]{2,1,0:T(8,128)(2,1)S(1)} collective-permute-done((bf16[2,384,512]{2,1,0:T(8,128)(2,1)S(1)}, bf16[2,384,512]{2,1,0:T(8,128)(2,1)S(1)}, u32[]{:S(2)}, u32[]{:S(2)}) %collective-permute-start.14) | collective-permute-done | bytes 786464 | tf_op jit(solution)/shard_map/ppermute | solution.py:259
  256.4 2.4 collective-permute-start.15
  258.9 3.2 %collective-permute-start.10 = (bf16[512,384]{1,0:T(8,128)(2,1)S(1)}, bf16[512,384]{1,0:T(8,128)(2,1)S(1)}, u32[]{:S(2)}, u32[]{:S(2)}) collective-permute-start(bf16[512,384]{1,0:T(8,128)(2,1)S(1)} %fusion.17), channel_id=1, source_target_pairs={{0,256},{256,0},{128,384},{384,128},{1,257},{257,1},{129,385},{385... | collective-permute-start | bytes 1179656 | tf_op jit(solution)/shard_map/ppermute | solution.py:237
  262.2 2.4 collective-permute-done.12
  265.4 7.6 %collective-permute-done.10 = bf16[512,384]{1,0:T(8,128)(2,1)S(1)} collective-permute-done((bf16[512,384]{1,0:T(8,128)(2,1)S(1)}, bf16[512,384]{1,0:T(8,128)(2,1)S(1)}, u32[]{:S(2)}, u32[]{:S(2)}) %collective-permute-start.10) | collective-permute-done | bytes 393248 | tf_op jit(solution)/shard_map/ppermute | solution.py:237
  (87 shorter events, 28.6 us)
Async XLA Ops:
  9.9 21.5 %copy-start.3 = (bf16[1,512,384]{2,1,0:T(8,128)(2,1)S(1)}, bf16[1,512,384]{2,1,0:T(8,128)(2,1)}, u32[]{:S(2)}) copy-start(bf16[1,512,384]{2,1,0:T(8,128)(2,1)} %param.13) | copy-start | bytes 1179652
  9.9 27.0 %copy-start.4 = (bf16[1,512,384]{2,1,0:T(8,128)(2,1)S(1)}, bf16[1,512,384]{2,1,0:T(8,128)(2,1)}, u32[]{:S(2)}) copy-start(bf16[1,512,384]{2,1,0:T(8,128)(2,1)} %param.14) | copy-start | bytes 1179652
  9.9 30.0 %copy-start.5 = (bf16[1,384,512]{2,1,0:T(8,128)(2,1)S(1)}, bf16[1,384,512]{2,1,0:T(8,128)(2,1)}, u32[]{:S(2)}) copy-start(bf16[1,384,512]{2,1,0:T(8,128)(2,1)} %param.15) | copy-start | bytes 1179652
  9.9 141.6 %all-to-all-start = ((bf16[128,8,2048]{2,1,0:T(8,128)(2,1)}), bf16[128,8,2048]{2,1,0:T(8,128)(2,1)}, u32[]{:S(2)}, u32[]{:S(2)}) async-start(bf16[128,8,2048]{2,1,0:T(8,128)(2,1)} %bitcast.74), calls=%async_computation | async-start | bytes 8388608 | tf_op jit(solution)/shard_map/all_to_all | solution.py:275
  31.4 97.7 %collective-permute-start.1 = (bf16[512,384]{1,0:T(8,128)(2,1)S(1)}, bf16[512,384]{1,0:T(8,128)(2,1)S(1)}, u32[]{:S(2)}, u32[]{:S(2)}) collective-permute-start(bf16[512,384]{1,0:T(8,128)(2,1)S(1)} %bitcast.76), channel_id=1, source_target_pairs={{0,256},{256,0},{128,384},{384,128},{1,257},{257,1},{129,385},{385... | collective-permute-start | bytes 1179656 | tf_op jit(solution)/shard_map/ppermute | solution.py:222
  33.8 99.8 %collective-permute-start = (bf16[512,384]{1,0:T(8,128)(2,1)S(1)}, bf16[512,384]{1,0:T(8,128)(2,1)S(1)}, u32[]{:S(2)}, u32[]{:S(2)}) collective-permute-start(bf16[512,384]{1,0:T(8,128)(2,1)S(1)} %bitcast.77), channel_id=1, source_target_pairs={{0,128},{128,0},{256,384},{384,256},{1,129},{129,1},{257,385},{385... | collective-permute-start | bytes 1179656 | tf_op jit(solution)/shard_map/ppermute | solution.py:223
  36.9 100.6 %collective-permute-start.4 = (bf16[512,384]{1,0:T(8,128)(2,1)S(1)}, bf16[512,384]{1,0:T(8,128)(2,1)S(1)}, u32[]{:S(2)}, u32[]{:S(2)}) collective-permute-start(bf16[512,384]{1,0:T(8,128)(2,1)S(1)} %bitcast.79), channel_id=1, source_target_pairs={{0,256},{256,0},{128,384},{384,128},{1,257},{257,1},{129,385},{385... | collective-permute-start | bytes 1179656 | tf_op jit(solution)/shard_map/ppermute | solution.py:222
  39.9 106.0 %collective-permute-start.7 = (bf16[384,512]{1,0:T(8,128)(2,1)S(1)}, bf16[384,512]{1,0:T(8,128)(2,1)S(1)}, u32[]{:S(2)}, u32[]{:S(2)}) collective-permute-start(bf16[384,512]{1,0:T(8,128)(2,1)S(1)} %bitcast.82), channel_id=1, source_target_pairs={{0,256},{256,0},{128,384},{384,128},{1,257},{257,1},{129,385},{385... | collective-permute-start | bytes 1179656 | tf_op jit(solution)/shard_map/ppermute | solution.py:222
  42.2 107.1 %collective-permute-start.3 = (bf16[512,384]{1,0:T(8,128)(2,1)S(1)}, bf16[512,384]{1,0:T(8,128)(2,1)S(1)}, u32[]{:S(2)}, u32[]{:S(2)}) collective-permute-start(bf16[512,384]{1,0:T(8,128)(2,1)S(1)} %bitcast.80), channel_id=1, source_target_pairs={{0,128},{128,0},{256,384},{384,256},{1,129},{129,1},{257,385},{385... | collective-permute-start | bytes 1179656 | tf_op jit(solution)/shard_map/ppermute | solution.py:223
  129.1 20.2 %collective-permute-start.6 = (bf16[384,512]{1,0:T(8,128)(2,1)S(1)}, bf16[384,512]{1,0:T(8,128)(2,1)S(1)}, u32[]{:S(2)}, u32[]{:S(2)}) collective-permute-start(bf16[384,512]{1,0:T(8,128)(2,1)S(1)} %bitcast.83), channel_id=1, source_target_pairs={{0,128},{128,0},{256,384},{384,256},{1,129},{129,1},{257,385},{385... | collective-permute-start | bytes 1179656 | tf_op jit(solution)/shard_map/ppermute | solution.py:223
  133.5 15.8 %collective-permute-start.2 = (bf16[512,384]{1,0:T(8,128)(2,1)S(1)}, bf16[512,384]{1,0:T(8,128)(2,1)S(1)}, u32[]{:S(2)}, u32[]{:S(2)}) collective-permute-start(bf16[512,384]{1,0:T(8,128)(2,1)S(1)} %collective-permute-done.1.refs_3_), channel_id=1, source_target_pairs={{0,128},{128,0},{256,384},{384,256},{1,129},{129,1},{257,385},{385... | collective-permute-start | bytes 1179656 | tf_op jit(solution)/shard_map/ppermute | solution.py:223
  137.5 12.6 %collective-permute-start.5 = (bf16[512,384]{1,0:T(8,128)(2,1)S(1)}, bf16[512,384]{1,0:T(8,128)(2,1)S(1)}, u32[]{:S(2)}, u32[]{:S(2)}) collective-permute-start(bf16[512,384]{1,0:T(8,128)(2,1)S(1)} %collective-permute-done.4.refs_7_), channel_id=1, source_target_pairs={{0,128},{128,0},{256,384},{384,256},{1,129},{129,1},{257,385},{385... | collective-permute-start | bytes 1179656 | tf_op jit(solution)/shard_map/ppermute | solution.py:223
  145.9 4.9 %collective-permute-start.8 = (bf16[384,512]{1,0:T(8,128)(2,1)S(1)}, bf16[384,512]{1,0:T(8,128)(2,1)S(1)}, u32[]{:S(2)}, u32[]{:S(2)}) collective-permute-start(bf16[384,512]{1,0:T(8,128)(2,1)S(1)} %collective-permute-done.7.refs_11_), channel_id=1, source_target_pairs={{0,128},{128,0},{256,384},{384,256},{1,129},{129,1},{257,385},{385... | collective-permute-start | bytes 1179656 | tf_op jit(solution)/shard_map/ppermute | solution.py:223
  169.0 20.8 %copy-start.16 = (bf16[512,384]{1,0:T(8,128)(2,1)S(1)}, bf16[512,384]{1,0:T(8,128)(2,1)}, u32[]{:S(2)}) copy-start(bf16[512,384]{1,0:T(8,128)(2,1)} %copy-done.15) | copy-start | bytes 1179652
  169.0 20.8 %copy-start.24 = (bf16[2,512,512]{2,1,0:T(8,128)(2,1)S(1)}, bf16[2,512,512]{2,1,0:T(8,128)(2,1)}, u32[]{:S(2)}) copy-start(bf16[2,512,512]{2,1,0:T(8,128)(2,1)} %get-tuple-element.23) | copy-start | bytes 3145732
  169.0 106.1 %all-to-all-start.1 = ((bf16[128,8,1024]{2,1,0:T(8,128)(2,1)}), bf16[128,8,1024]{2,1,0:T(8,128)(2,1)S(1)}, u32[]{:S(2)}, u32[]{:S(2)}) async-start(bf16[128,8,1024]{2,1,0:T(8,128)(2,1)} %bitcast.88), calls=%async_computation.1 | async-start | bytes 4194304 | tf_op jit(solution)/shard_map/all_to_all | solution.py:275
  190.6 11.3 %collective-permute-start.13 = (bf16[2,384,512]{2,1,0:T(8,128)(2,1)S(1)}, bf16[2,384,512]{2,1,0:T(8,128)(2,1)S(1)}, u32[]{:S(2)}, u32[]{:S(2)}) collective-permute-start(bf16[2,384,512]{2,1,0:T(8,128)(2,1)S(1)} %pad_maximum_fusion), channel_id=1, source_target_pairs={{0,128},{128,0},{256,384},{384,256},{1,129},{129,1},{257,385},{385... | collective-permute-start | bytes 2359304 | tf_op jit(solution)/shard_map/ppermute | solution.py:257
  194.8 5.6 %copy-start.25 = (bf16[2,512,512]{2,1,0:T(8,128)(2,1)S(1)}, bf16[2,512,512]{2,1,0:T(8,128)(2,1)}, u32[]{:S(2)}) copy-start(bf16[2,512,512]{2,1,0:T(8,128)(2,1)} %get-tuple-element.17) | copy-start | bytes 3145732
  195.7 10.6 %collective-permute-start.11 = (bf16[2,512,384]{2,1,0:T(8,128)(2,1)S(1)}, bf16[2,512,384]{2,1,0:T(8,128)(2,1)S(1)}, u32[]{:S(2)}, u32[]{:S(2)}) collective-permute-start(bf16[2,512,384]{2,1,0:T(8,128)(2,1)S(1)} %convolution_convert_fusion), channel_id=1, source_target_pairs={{0,128},{128,0},{256,384},{384,256},{1,129},{129,1},{257,385},{385... | collective-permute-start | bytes 2359304 | tf_op jit(solution)/shard_map/ppermute | solution.py:235
  197.7 10.8 %collective-permute-start.9 = (bf16[2,512,384]{2,1,0:T(8,128)(2,1)S(1)}, bf16[2,512,384]{2,1,0:T(8,128)(2,1)S(1)}, u32[]{:S(2)}, u32[]{:S(2)}) collective-permute-start(bf16[2,512,384]{2,1,0:T(8,128)(2,1)S(1)} %convolution_convert_fusion.2), channel_id=1, source_target_pairs={{0,128},{128,0},{256,384},{384,256},{1,129},{129,1},{257,385},{385... | collective-permute-start | bytes 2359304 | tf_op jit(solution)/shard_map/ppermute | solution.py:235
  202.2 53.9 %collective-permute-start.14 = (bf16[2,384,512]{2,1,0:T(8,128)(2,1)S(1)}, bf16[2,384,512]{2,1,0:T(8,128)(2,1)S(1)}, u32[]{:S(2)}, u32[]{:S(2)}) collective-permute-start(bf16[2,384,512]{2,1,0:T(8,128)(2,1)S(1)} %add_convert_fusion.1), channel_id=1, source_target_pairs={{0,256},{256,0},{128,384},{384,128},{1,257},{257,1},{129,385},{385... | collective-permute-start | bytes 2359304 | tf_op jit(solution)/shard_map/ppermute | solution.py:259
  206.6 58.0 %collective-permute-start.12 = (bf16[512,384]{1,0:T(8,128)(2,1)S(1)}, bf16[512,384]{1,0:T(8,128)(2,1)S(1)}, u32[]{:S(2)}, u32[]{:S(2)}) collective-permute-start(bf16[512,384]{1,0:T(8,128)(2,1)S(1)} %fusion.19), channel_id=1, source_target_pairs={{0,256},{256,0},{128,384},{384,128},{1,257},{257,1},{129,385},{385... | collective-permute-start | bytes 1179656 | tf_op jit(solution)/shard_map/ppermute | solution.py:237
  256.4 17.3 %collective-permute-start.15 = (bf16[2,384,512]{2,1,0:T(8,128)(2,1)S(1)}, bf16[2,384,512]{2,1,0:T(8,128)(2,1)S(1)}, u32[]{:S(2)}, u32[]{:S(2)}) collective-permute-start(bf16[2,384,512]{2,1,0:T(8,128)(2,1)S(1)} %add_convert_fusion.even_ref), channel_id=1, source_target_pairs={{0,128},{128,0},{256,384},{384,256},{1,129},{129,1},{257,385},{385... | collective-permute-start | bytes 2359304 | tf_op jit(solution)/shard_map/ppermute | solution.py:261
  258.9 14.0 %collective-permute-start.10 = (bf16[512,384]{1,0:T(8,128)(2,1)S(1)}, bf16[512,384]{1,0:T(8,128)(2,1)S(1)}, u32[]{:S(2)}, u32[]{:S(2)}) collective-permute-start(bf16[512,384]{1,0:T(8,128)(2,1)S(1)} %fusion.17), channel_id=1, source_target_pairs={{0,256},{256,0},{128,384},{384,128},{1,257},{257,1},{129,385},{385... | collective-permute-start | bytes 1179656 | tf_op jit(solution)/shard_map/ppermute | solution.py:237
  (21 other events, 26.6 us)

commit v2 on v1

v2 whole, which is shorter than its diff:
```python
import functools

import jax
import jax.numpy as jnp
from jax import lax
from jax.experimental import pallas as pl
from jax.experimental.pallas import tpu as pltpu
from jax.sharding import PartitionSpec as P

BF16 = jnp.bfloat16
F32 = jnp.float32
I32 = jnp.int32
VMEM = 56 << 20
SMALL = 24 << 20
AXES = ("dp", "expert", "seq")

OTHER_CORE = [(0, 1), (1, 0), (2, 3), (3, 2)]
OTHER_CHIP = [(0, 2), (2, 0), (1, 3), (3, 1)]


def iota(shape, dim):
    return lax.broadcasted_iota(I32, shape, dim)


def as_bf16(mask):
    return jnp.where(mask, 1.0, 0.0).astype(BF16)


def dot(a, b):
    return jnp.dot(a, b, preferred_element_type=F32)


def add(a, b):
    return a.astype(F32) + b.astype(F32)


def vmem():
    return pl.BlockSpec(memory_space=pltpu.VMEM)


def smem():
    return pl.BlockSpec(memory_space=pltpu.SMEM)


def anywhere():
    return pl.BlockSpec(memory_space=pl.ANY)


def cost(flops, moved, transcendentals=0):
    return pl.CostEstimate(flops=flops, bytes_accessed=moved, transcendentals=transcendentals)


def shaped(*shape, dtype=BF16):
    return jax.ShapeDtypeStruct(shape, dtype)


def local(kernel, outs, *args, scalars=0, moved=4 << 20, flops=0):
    return pl.pallas_call(
        kernel,
        in_specs=[smem()] * scalars + [vmem()] * (len(args) - scalars),
        out_specs=[vmem()] * len(outs),
        out_shape=outs,
        compiler_params=pltpu.CompilerParams(vmem_limit_bytes=SMALL),
        cost_estimate=cost(flops, moved),
    )(*args)


def send_kernel(experts, cap, ids_ref, weight_ref, scale_ref, codes_ref, grad_ref, send_ref, row_ref, table, place):
    step = pl.program_id(0)
    tokens, features = codes_ref.shape
    rows = send_ref.shape[0]

    @pl.when(step == 0)
    def _():
        ids = ids_ref[...]
        expert = iota((experts, tokens), 0)
        first, second = expert == ids[0:1, :], expert == ids[1:2, :]
        earlier = as_bf16(iota((tokens, tokens), 0) < iota((tokens, tokens), 1))
        count = dot(as_bf16(first | second), earlier)
        rank0 = jnp.sum(jnp.where(first, count, 0.0), axis=0, keepdims=True)
        rank1 = jnp.sum(jnp.where(second, count, 0.0), axis=0, keepdims=True)
        row0 = 2 * cap * ids[0:1, :] + rank0.astype(I32)
        row1 = 2 * cap * ids[1:2, :] + rank1.astype(I32)
        place[0:1, :] = row0
        place[1:2, :] = row1
        both = jnp.concatenate([row0.astype(F32), row1.astype(F32), jnp.zeros((tokens - 2, tokens), F32)], axis=0)
        row_ref[...] = both.T.astype(I32)
        blocks = scale_ref.shape[0]
        scale = jnp.concatenate([scale_ref[...], jnp.zeros((tokens - blocks, tokens), F32)], axis=0).T
        lanes = features // blocks
        for j in range(blocks):
            part = slice(j * lanes, (j + 1) * lanes)
            table[0:tokens, part] = (codes_ref[:, part].astype(F32) * scale[:, j : j + 1]).astype(BF16)
        table[tokens : 2 * tokens, :] = grad_ref[...]

    row = iota((rows, tokens), 0) + step * rows
    is_grad = (row & cap) != 0
    base = row - (row & cap)
    in0, in1 = base == place[0:1, :], base == place[1:2, :]
    weight = jnp.sum(
        jnp.where(in0, weight_ref[0:1, :], 0.0) + jnp.where(in1, weight_ref[1:2, :], 0.0), axis=1, keepdims=True
    )
    weight = jnp.where(is_grad[:, 0:1], weight, 1.0)
    inside = in0 | in1
    pick = jnp.concatenate([as_bf16(inside & jnp.logical_not(is_grad)), as_bf16(inside & is_grad)], axis=1)
    width = 512
    for start in range(0, features, width):
        part = slice(start, start + width)
        send_ref[:, part] = (dot(pick, table[:, part]) * weight).astype(BF16)


def rows_to_send(ids, weights, scales, codes, grads, experts, cap):
    tokens, features = codes.shape
    total = 2 * experts * cap
    rows = 256
    whole = lambda a: pl.BlockSpec(a.shape, lambda i: (0, 0))
    return pl.pallas_call(
        functools.partial(send_kernel, experts, cap),
        grid=(total // rows,),
        in_specs=[whole(a) for a in (ids, weights, scales, codes, grads)],
        out_specs=[pl.BlockSpec((rows, features), lambda i: (i, 0)), pl.BlockSpec((tokens, tokens), lambda i: (0, 0))],
        out_shape=[shaped(total, features), shaped(tokens, tokens, dtype=I32)],
        scratch_shapes=[pltpu.VMEM((2 * tokens, features), BF16), pltpu.VMEM((8, tokens), I32)],
        compiler_params=pltpu.CompilerParams(vmem_limit_bytes=VMEM),
        cost_estimate=cost(1 << 38, 6 << 20),
    )(ids, weights, scales, codes, grads)


def pack_kernel(gate, up, down, out):
    out[0] = gate[...]
    out[1] = up[...]
    out[2] = down[...].T


def merge_kernel(own, chip, out):
    out[0] = own[...]
    out[1] = chip[...]


def arrange_kernel(dp_ref, mine, theirs, pre_mat, down_mat, back_mat):
    width, hid = mine.shape[2:]
    for r, ref in enumerate((mine, theirs, mine, theirs)):
        at = pl.ds(pl.multiple_of((dp_ref[0] ^ r) * width, width), width)
        for k in range(2):
            value = ref[r // 2, k]
            pre_mat[at, k * hid : (k + 1) * hid] = value
            back_mat[k * hid : (k + 1) * hid, at] = value.T
        down_mat[at, :] = ref[r // 2, 2]


def expert_weights(gate, up, down, dp):
    width, hid = gate.shape
    (own,) = local(pack_kernel, [shaped(3, width, hid)], gate, up, down)
    chip = lax.ppermute(own, "dp", OTHER_CHIP)
    (mine,) = local(merge_kernel, [shaped(2, 3, width, hid)], own, chip, flops=1 << 38)
    theirs = lax.ppermute(mine, "dp", OTHER_CORE)
    full = 4 * width
    return local(
        arrange_kernel,
        [shaped(full, 2 * hid), shaped(full, hid), shaped(2 * hid, full)],
        dp,
        mine,
        theirs,
        scalars=1,
        moved=12 << 20,
    )


def chunk_row(cap, rows, index):
    half = rows // 2
    slot = index & (half - 1)
    row = (slot // cap) * (2 * cap) + (slot & (cap - 1))
    return jnp.where(index >= half, row + cap, row)


def gather_matrix(cap, rows):
    return as_bf16(iota((rows, rows), 1) == chunk_row(cap, rows, iota((rows, rows), 0)))


def spread_matrix(cap, rows):
    return as_bf16(iota((rows, rows), 0) == chunk_row(cap, rows, iota((rows, rows), 1)))


def expert_kernel(
    cap, recv, pre_mat, down_mat, back_mat, back, x_out, dy_out, d_gu, hidden, landed, x, dy, pre, d_hid, dx, recv_sem, out_sem
):
    slots, features = x.shape
    hid = hidden.shape[1]
    blocks, block = landed.shape[:2]
    half = block // 2
    width = 512

    arrivals = [
        pltpu.make_async_copy(recv.at[pl.ds(b * block, block)], landed.at[b], recv_sem.at[b]) for b in range(blocks)
    ]
    for copy in arrivals:
        copy.start()
    gather = gather_matrix(cap, block)
    for b in range(blocks):
        arrivals[b].wait()
        at = slice(b * half, (b + 1) * half)
        for start in range(0, features, width):
            part = slice(start, start + width)
            rows = dot(gather, landed[b, :, part]).astype(BF16)
            x[at, part] = rows[:half]
            dy[at, part] = rows[half:]
    departures = [pltpu.make_async_copy(x, x_out, out_sem.at[0]), pltpu.make_async_copy(dy, dy_out, out_sem.at[1])]
    for copy in departures:
        copy.start()

    pre[...] = dot(x[...], pre_mat[...])
    d_hid[...] = dot(dy[...], down_mat[...])

    step = 64

    @pl.loop(0, slots // step)
    def _(i):
        at = pl.ds(pl.multiple_of(i * step, step), step)
        pg, pu, dh = pre[at, 0:hid], pre[at, hid : 2 * hid], d_hid[at, :]
        sig = jax.nn.sigmoid(pg)
        act = pg * sig
        hidden[at, :] = (act * pu).astype(BF16)
        d_gu[at, 0:hid] = (dh * pu * sig * (1.0 + pg * (1.0 - sig))).astype(BF16)
        d_gu[at, hid : 2 * hid] = (dh * act).astype(BF16)

    for start in range(0, features, width):
        part = slice(start, start + width)
        dx[:, part] = dot(d_gu[...], back_mat[:, part]).astype(BF16)
    spread = spread_matrix(cap, block)
    for b in range(blocks):
        at = slice(b * half, (b + 1) * half)
        for start in range(0, features // 2, width):
            low, high = slice(start, start + width), slice(features // 2 + start, features // 2 + start + width)
            rows = jnp.concatenate([dx[at, low], dx[at, high]], axis=0)
            back[b * block : (b + 1) * block, low] = dot(spread, rows).astype(BF16)
    for copy in departures:
        copy.wait()


def expert_rows(recv, pre_mat, down_mat, back_mat, cap):
    total, features = recv.shape
    slots = total // 2
    hid = down_mat.shape[1]
    block = 256
    return pl.pallas_call(
        functools.partial(expert_kernel, cap),
        in_specs=[anywhere()] + [vmem()] * 3,
        out_specs=[vmem()] + [anywhere()] * 2 + [vmem()] * 2,
        out_shape=[
            shaped(total, features // 2),
            shaped(slots, features),
            shaped(slots, features),
            shaped(slots, 2 * hid),
            shaped(slots, hid),
        ],
        scratch_shapes=[
            pltpu.VMEM((total // block, block, features), BF16),
            pltpu.VMEM((slots, features), BF16),
            pltpu.VMEM((slots, features), BF16),
            pltpu.VMEM((slots, 2 * hid), F32),
            pltpu.VMEM((slots, hid), F32),
            pltpu.VMEM((slots, features), BF16),
            pltpu.SemaphoreType.DMA((total // block,)),
            pltpu.SemaphoreType.DMA((2,)),
        ],
        compiler_params=pltpu.CompilerParams(vmem_limit_bytes=VMEM),
        cost_estimate=cost(2 * slots * features * hid * 5, 16 << 20, slots * hid),
    )(recv, pre_mat, down_mat, back_mat)


def odd_kernel(dp_ref, x, dy, d_gu, hidden, out, turned_out, turned):
    @pl.when(pl.program_id(0) == 0)
    def _():
        wide = d_gu.shape[1]
        turned[0:wide, :] = d_gu[...].T
        turned[wide:, :] = hidden[...].T
        turned_out[...] = turned[...]

    even_kernel(dp_ref, x, dy, turned, out)


def even_kernel(dp_ref, x, dy, turned, out):
    hid = out.shape[1]
    for k, rows in enumerate((x, x, dy)):
        out[k] = dot(turned[k * hid : (k + 1) * hid, :], rows[...]).astype(BF16)


def partial_grads(kernel, first, dp, x, dy, grads, outs, scratch):
    slots, features = x.shape
    width = features // 4
    rows = pl.BlockSpec((slots, width), lambda i, dp: (0, dp[0] ^ (2 * i + first)))
    whole = lambda a: pl.BlockSpec(a.shape, lambda i, dp: (0, 0))
    hid = outs[0].shape[2]
    return pl.pallas_call(
        kernel,
        grid_spec=pltpu.PrefetchScalarGridSpec(
            num_scalar_prefetch=1,
            grid=(2,),
            in_specs=[rows, rows] + [whole(g) for g in grads],
            out_specs=[pl.BlockSpec((None, 3, hid, width), lambda i, dp: (i, 0, 0, 0))] + [whole(o) for o in outs[1:]],
            scratch_shapes=scratch,
        ),
        out_shape=outs,
        compiler_params=pltpu.CompilerParams(vmem_limit_bytes=VMEM),
        cost_estimate=cost(12 * slots * width * hid, 6 << 20),
    )(dp, x, dy, *grads)


def first_kernel(even, given, down, gate_up, keep):
    for r in range(2):
        down[r] = add(even[r, 2], given[r, 2]).astype(BF16)
    for k in range(2):
        gate_up[k] = add(even[1, k], given[1, k]).astype(BF16)
        keep[k] = add(even[0, k], given[0, k]).astype(BF16)


def down_kernel(sent, other, out):
    out[0] = add(sent[0], other[1]).astype(BF16)
    out[1] = add(sent[1], other[0]).astype(BF16)


def gate_up_kernel(keep, other, gate, up):
    gate[...] = add(keep[0], other[0]).astype(BF16).T
    up[...] = add(keep[1], other[1]).astype(BF16).T


def place_kernel(dp_ref, even, odd, out):
    width = even.shape[2]
    for r, ref in enumerate((even, odd, even, odd)):
        out[:, pl.ds(pl.multiple_of((dp_ref[0] ^ r) * width, width), width)] = ref[r // 2]


def summed_grads(x, dy, d_gu, hidden, dp):
    slots, features = x.shape
    width, hid = features // 4, hidden.shape[1]
    part = shaped(2, 3, hid, width)
    turned = shaped(3 * hid, slots)
    odd, grads = partial_grads(
        odd_kernel, 1, dp, x, dy, (d_gu, hidden), [part, turned], [pltpu.VMEM(turned.shape, BF16)]
    )
    given = lax.ppermute(odd, "dp", OTHER_CORE)
    (even,) = partial_grads(even_kernel, 0, dp, x, dy, (grads,), [part], [])
    two = shaped(2, hid, width)
    down, gate_up, keep = local(first_kernel, [two] * 3, even, given)
    down_other = lax.ppermute(down, "dp", OTHER_CHIP)
    gate_up_other = lax.ppermute(gate_up, "dp", OTHER_CHIP)
    (mine,) = local(down_kernel, [two], down, down_other)
    theirs = lax.ppermute(mine, "dp", OTHER_CORE)
    (grad_down,) = local(place_kernel, [shaped(hid, features)], dp, mine, theirs, scalars=1)
    grad_gate, grad_up = local(gate_up_kernel, [shaped(width, hid)] * 2, keep, gate_up_other)
    return grad_gate, grad_up, grad_down


def token_kernel(cap, row_ref, recv_ref, out_ref):
    tokens, features = out_ref.shape
    total, half = recv_ref.shape
    row0, row1 = row_ref[:, 0:1], row_ref[:, 1:2]
    at = iota((tokens, total), 1)
    low = as_bf16((at == row0) | (at == row1))
    high = as_bf16((at == row0 + cap) | (at == row1 + cap))
    width = 512
    for p, pick in enumerate((low, high)):
        for start in range(0, half, width):
            value = dot(pick, recv_ref[:, start : start + width])
            out_ref[:, p * half + start : p * half + start + width] = value.astype(BF16)


def token_rows(row_of, recv, tokens, features, cap):
    return pl.pallas_call(
        functools.partial(token_kernel, cap),
        in_specs=[vmem(), vmem()],
        out_specs=vmem(),
        out_shape=shaped(tokens, features),
        compiler_params=pltpu.CompilerParams(vmem_limit_bytes=SMALL),
        cost_estimate=cost(4 * tokens * features * recv.shape[0], 3 << 20),
    )(row_of, recv)


def exchange(rows, experts):
    near = experts // 2
    members = [
        [(2 * (chip ^ (e // near)) + core) * experts + e for e in range(experts)] for chip in range(2) for core in range(2)
    ]
    chunks = rows.reshape(experts, rows.shape[0] // experts, rows.shape[1])
    moved = lax.all_to_all(chunks, AXES, split_axis=0, concat_axis=0, axis_index_groups=members, tiled=True)
    return moved.reshape(rows.shape)


def per_device(codes, scales, grad_out, route_weight, expert_ids, w_gate, w_up, w_down):
    tokens, features = codes.shape
    experts = lax.axis_size("expert") * lax.axis_size("seq")
    cap = 2 * tokens * expert_ids.shape[1] // experts
    dp = lax.axis_index("dp").astype(I32).reshape(1)
    mats = expert_weights(w_gate[0], w_up[0], w_down[0], dp)
    send, row_of = rows_to_send(expert_ids.T, route_weight.T, scales.T, codes, grad_out, experts, cap)
    recv = exchange(send, experts)
    back, x, dy, d_gu, hidden = expert_rows(recv, *mats, cap)
    returned = exchange(back, experts)
    grad_gate, grad_up, grad_down = summed_grads(x, dy, d_gu, hidden, dp)
    grad_input = token_rows(row_of, returned, tokens, features, cap)
    return grad_input, grad_gate[None], grad_up[None], grad_down[None]


def solution(mesh):
    rows = P(AXES, None)
    split = P(("expert", "seq"), "dp", None)
    return jax.shard_map(
        per_device,
        mesh=mesh,
        in_specs=(rows, rows, rows, rows, rows, split, split, P(("expert", "seq"), None, "dp")),
        out_specs=(rows, split, split, P(("expert", "seq"), None, None)),
        check_vma=False,
    )
```

time: 279 us -> 263 us (0.943)
  Pallas kernels: 17.5 us -> 39.3 us
  starting transfers between devices: 88.3 us -> 72.5 us
  waiting for transfers between devices: 148 us -> 138 us
  local copies, waits for them, and re-layouts: 14.8 us -> 9.21 us
  matrix products: 4.55 us -> 0 us
    ppermute x16 -> x6, waiting for transfers between devices: 148 us -> 49.8 us  [the longest x1 34.7 us: summed_grads(): down_other = lax.ppermute(down, 'dp', OTHER_CHIP)]
    all_to_all x2, waiting for transfers between devices: 0.01 us -> 88.2 us  [exchange(): lax.all_to_all(chunks, AXES, split_axis=0, concat_axis=0, axis_index_grou...]
    pallas_call x3 -> x11, Pallas kernels: 15 us -> 34 us  [the longest x1 14.7 us: expert_rows(): pl.pallas_call(functools.partial(expert_kernel, cap), in_specs=[anywhere(...]
    ppermute x16 -> x6, starting transfers between devices: 46.1 us -> 28.2 us  [the longest x1 8 us: expert_weights(): theirs = lax.ppermute(mine, 'dp', OTHER_CORE)]
    unnamed x54 -> x16, local copies, waits for them, and re-layouts: 14.7 us -> 9.21 us
    dot_general x8 -> x0, matrix products: 4.55 us -> none  [the longest x4 2.97 us: partial_sum(): lax.dot_general(blocks, grads, (((1,), (0,)), ((), ())), preferred_elemen...]
    pallas_call x1, Pallas kernels: 2.48 us -> 5.31 us  [rows_to_send(): pl.pallas_call(functools.partial(send_kernel, experts, cap), grid=(total...]
  transfers between devices with their start and end apart: 18 -> 8, of which waited for: 6 -> 5; matrix products, arithmetic and copies ran while one was open for 3% -> 0% of each run, Pallas kernels for 0% -> 8%
where the time goes in v2:
time: 263 us; the launch traced here: 260 us
  waiting for transfers between devices  138 us (52%)
  starting transfers between devices  72.5 us (28%)
  Pallas kernels  39.3 us (15%)
  local copies, waits for them, and re-layouts  9.21 us (4%)
    all_to_all x2, waiting for transfers between devices, exchange(): lax.all_to_all(chunks, AXES, split_axis=0, concat_axis=0, axis_index_grou...  88.2 us
    all_to_all x2, starting transfers between devices, exchange(): lax.all_to_all(chunks, AXES, split_axis=0, concat_axis=0, axis_index_grou...  44.3 us
    ppermute x1, waiting for transfers between devices, summed_grads(): down_other = lax.ppermute(down, 'dp', OTHER_CHIP)  34.7 us
    pallas_call x1, Pallas kernels, expert_rows(): pl.pallas_call(functools.partial(expert_kernel, cap), in_specs=[anywhere(...  14.7 us
    ppermute x1, waiting for transfers between devices, summed_grads(): gate_up_other = lax.ppermute(gate_up, 'dp', OTHER_CHIP)  10.7 us
    unnamed x16, local copies, waits for them, and re-layouts  9.21 us
    pallas_call x7, Pallas kernels, local(): pl.pallas_call(kernel, in_specs=[smem()] * scalars + [vmem()] * (len(args...  8.9 us
    pallas_call x2, Pallas kernels, partial_grads(): pl.pallas_call(kernel, grid_spec=pltpu.PrefetchScalarGridSpec(num_scalar_...  8.86 us
  transfers between devices with their start and end apart: 8, of which 5 were waited for; matrix products, arithmetic and copies ran while one was open for 0% of the time, Pallas kernels for 8%

profile of v2, /device:TPU:1, one launch (start us, length us, event | category | flops | bytes accessed | tf_op | source)
XLA Modules:
  0.0 259.9 jit_solution(13376171810206436151)
XLA Ops:
  3.6 1.2 shard_map.112.own
  4.8 4.0 %collective-permute-start = (bf16[3,512,384]{2,1,0:T(8,128)(2,1)}, bf16[3,512,384]{2,1,0:T(8,128)(2,1)}, u32[]{:S(2)}, u32[]{:S(2)}) collective-permute-start(bf16[3,512,384]{2,1,0:T(8,128)(2,1)} %shard_map.112.own), channel_id=1, source_target_pairs={{0,256},{256,0},{128,384},{384,128},{1,257},{257,1},{129,385},{385... | collective-permute-start | bytes 3538952 | tf_op jit(solution)/shard_map/ppermute | solution.py:154
  8.8 5.3 %shard_map.111 = (bf16[1024,2048]{1,0:T(8,128)(2,1)}, s32[128,128]{1,0:T(8,128)}) custom-call(s32[2,128]{1,0:T(2,128)} %bitcast.24, f32[2,128]{1,0:T(2,128)} %bitcast.25, f32[16,128]{1,0:T(8,128)} %bitcast.23, bf16[128,2048]{1,0:T(8,128)(2,1)} %codes_ref.1, bf16[128,2048]{1,0:T(8,128)(2,1)} %grad_ref.1), custom_call_target="tpu_custom_call" | custom-call | flops 274877906944 | bytes 6291456 | tf_op jit(solution)/shard_map/pallas_call | solution.py:117
  14.2 19.5 %all-to-all-start = ((bf16[128,8,2048]{2,1,0:T(8,128)(2,1)}), bf16[128,8,2048]{2,1,0:T(8,128)(2,1)}, u32[]{:S(2)}, u32[]{:S(2)}) async-start(bf16[128,8,2048]{2,1,0:T(8,128)(2,1)} %bitcast.18), calls=%async_computation | async-start | bytes 8388608 | tf_op jit(solution)/shard_map/all_to_all | solution.py:385
  33.7 1.8 shard_map.113.mine
  35.5 8.0 %collective-permute-start.1 = (bf16[2,3,512,384]{3,2,1,0:T(8,128)(2,1)S(1)}, bf16[2,3,512,384]{3,2,1,0:T(8,128)(2,1)}, u32[]{:S(2)}, u32[]{:S(2)}) collective-permute-start(bf16[2,3,512,384]{3,2,1,0:T(8,128)(2,1)S(1)} %shard_map.113.mine), channel_id=1, source_target_pairs={{0,128},{128,0},{256,384},{384,256},{1,129},{129,1},{257,385},{385... | collective-permute-start | bytes 7077896 | tf_op jit(solution)/shard_map/ppermute | solution.py:156
  43.5 4.3 %collective-permute-done.1.theirs = bf16[2,3,512,384]{3,2,1,0:T(8,128)(2,1)} collective-permute-done((bf16[2,3,512,384]{3,2,1,0:T(8,128)(2,1)S(1)}, bf16[2,3,512,384]{3,2,1,0:T(8,128)(2,1)}, u32[]{:S(2)}, u32[]{:S(2)}) %collective-permute-start.1) | collective-permute-done | bytes 2359328 | tf_op jit(solution)/shard_map/ppermute | solution.py:156
  47.8 2.9 %shard_map.114 = (bf16[2048,768]{1,0:T(8,128)(2,1)S(1)}, bf16[2048,384]{1,0:T(8,128)(2,1)S(1)}, bf16[768,2048]{1,0:T(8,128)(2,1)S(1)}) custom-call(s32[1]{0:T(128)} %bitcast.5.dp_ref, bf16[2,3,512,384]{3,2,1,0:T(8,128)(2,1)S(1)} %shard_map.113.mine, bf16[2,3,512,384]{3,2,1,0:T(8,128)(2,1)} %collective-permute-done.1.theirs), custom_call_target="tpu_custom_call" | custom-call | bytes 12582912 | tf_op jit(solution)/shard_map/pallas_call | solution.py:58
  50.7 1.8 copy-done.4
  52.5 1.6 copy-done.5
  55.2 88.2 %all-to-all-done = bf16[128,8,2048]{2,1,0:T(8,128)(2,1)} async-done(((bf16[128,8,2048]{2,1,0:T(8,128)(2,1)}), bf16[128,8,2048]{2,1,0:T(8,128)(2,1)}, u32[]{:S(2)}, u32[]{:S(2)}) %all-to-all-start) | async-done | bytes 4194336 | tf_op jit(solution)/shard_map/all_to_all | solution.py:385
  143.5 14.7 %shard_map.115 = (bf16[1024,1024]{1,0:T(8,128)(2,1)}, bf16[512,2048]{1,0:T(8,128)(2,1)}, bf16[512,2048]{1,0:T(8,128)(2,1)}, bf16[512,768]{1,0:T(8,128)(2,1)}, bf16[512,384]{1,0:T(8,128)(2,1)}) custom-call(bf16[1024,2048]{1,0:T(8,128)(2,1)} %bitcast.4.recv, bf16[2048,768]{1,0:T(8,128)(2,1)} %copy-done.4, bf16[2048,384]{1,0:T(8,128)(2,1)} %copy-done.6, ...), custom_call_target="tpu_custom_call" | custom-call | flops 4026531840 | bytes 16777216 | tf_op jit(solution)/shard_map/pallas_call | solution.py:245
  158.1 24.8 %all-to-all-start.1 = ((bf16[128,8,1024]{2,1,0:T(8,128)(2,1)}), bf16[128,8,1024]{2,1,0:T(8,128)(2,1)S(1)}, u32[]{:S(2)}, u32[]{:S(2)}) async-start(bf16[128,8,1024]{2,1,0:T(8,128)(2,1)} %bitcast.19), calls=%async_computation.1 | async-start | bytes 4194304 | tf_op jit(solution)/shard_map/all_to_all | solution.py:385
  183.0 4.6 %shard_map.117 = (bf16[2,3,384,512]{3,2,1,0:T(8,128)(2,1)}, bf16[1152,512]{1,0:T(8,128)(2,1)}) custom-call(s32[1]{0:T(128)} %bitcast.5.dp_ref, bf16[512,2048]{1,0:T(8,128)(2,1)} %get-tuple-element.27.x, bf16[512,2048]{1,0:T(8,128)(2,1)} %get-tuple-element.28.dy, bf16[512,768]{1,0:T(8,128)(2,1)} %get-tuple-element.29.d_gu, ...), custom_call_target="tpu_custom_call" | custom-call | flops 1207959552 | bytes 6291456 | tf_op jit(solution)/shard_map/pallas_call | solution.py:294
  187.6 5.0 %collective-permute-start.2 = (bf16[2,3,384,512]{3,2,1,0:T(8,128)(2,1)}, bf16[2,3,384,512]{3,2,1,0:T(8,128)(2,1)S(1)}, u32[]{:S(2)}, u32[]{:S(2)}) collective-permute-start(bf16[2,3,384,512]{3,2,1,0:T(8,128)(2,1)} %get-tuple-element.32), channel_id=1, source_target_pairs={{0,128},{128,0},{256,384},{384,256},{1,129},{129,1},{257,385},{385... | collective-permute-start | bytes 7077896 | tf_op jit(solution)/shard_map/ppermute | solution.py:341
  192.6 4.3 %shard_map.118.even = bf16[2,3,384,512]{3,2,1,0:T(8,128)(2,1)} custom-call(s32[1]{0:T(128)} %bitcast.5.dp_ref, bf16[512,2048]{1,0:T(8,128)(2,1)} %get-tuple-element.27.x, bf16[512,2048]{1,0:T(8,128)(2,1)} %get-tuple-element.28.dy, bf16[1152,512]{1,0:T(8,128)(2,1)} %get-tuple-element.31.turned), custom_call_target="tpu_custom_call" | custom-call | flops 1207959552 | bytes 6291456 | tf_op jit(solution)/shard_map/pallas_call | solution.py:294
  196.9 1.7 copy-done
  199.1 1.9 collective-permute-start.4
  201.0 3.4 %collective-permute-start.3 = (bf16[2,384,512]{2,1,0:T(8,128)(2,1)S(1)}, bf16[2,384,512]{2,1,0:T(8,128)(2,1)S(1)}, u32[]{:S(2)}, u32[]{:S(2)}) collective-permute-start(bf16[2,384,512]{2,1,0:T(8,128)(2,1)S(1)} %get-tuple-element.34), channel_id=1, source_target_pairs={{0,256},{256,0},{128,384},{384,128},{1,257},{257,1},{129,385},{385... | collective-permute-start | bytes 2359304 | tf_op jit(solution)/shard_map/ppermute | solution.py:346
  204.4 34.7 %collective-permute-done.4.other = bf16[2,384,512]{2,1,0:T(8,128)(2,1)S(1)} collective-permute-done((bf16[2,384,512]{2,1,0:T(8,128)(2,1)S(1)}, bf16[2,384,512]{2,1,0:T(8,128)(2,1)S(1)}, u32[]{:S(2)}, u32[]{:S(2)}) %collective-permute-start.4) | collective-permute-done | bytes 786464 | tf_op jit(solution)/shard_map/ppermute | solution.py:345
  239.3 5.9 %collective-permute-start.5 = (bf16[2,384,512]{2,1,0:T(8,128)(2,1)S(1)}, bf16[2,384,512]{2,1,0:T(8,128)(2,1)S(1)}, u32[]{:S(2)}, u32[]{:S(2)}) collective-permute-start(bf16[2,384,512]{2,1,0:T(8,128)(2,1)S(1)} %shard_map.121.even), channel_id=1, source_target_pairs={{0,128},{128,0},{256,384},{384,256},{1,129},{129,1},{257,385},{385... | collective-permute-start | bytes 2359304 | tf_op jit(solution)/shard_map/ppermute | solution.py:348
  245.2 10.7 %collective-permute-done.3.other = bf16[2,384,512]{2,1,0:T(8,128)(2,1)S(1)} collective-permute-done((bf16[2,384,512]{2,1,0:T(8,128)(2,1)S(1)}, bf16[2,384,512]{2,1,0:T(8,128)(2,1)S(1)}, u32[]{:S(2)}, u32[]{:S(2)}) %collective-permute-start.3) | collective-permute-done | bytes 786464 | tf_op jit(solution)/shard_map/ppermute | solution.py:346
  257.0 1.3 shard_map.122
  258.3 1.6 shard_map.116
  (20 shorter events, 5.9 us)
Async XLA Ops:
  0.6 1.0 copy-start.1
  1.6 1.0 copy-start.2
  2.6 1.0 copy-start.3
  4.8 28.9 %collective-permute-start = (bf16[3,512,384]{2,1,0:T(8,128)(2,1)}, bf16[3,512,384]{2,1,0:T(8,128)(2,1)}, u32[]{:S(2)}, u32[]{:S(2)}) collective-permute-start(bf16[3,512,384]{2,1,0:T(8,128)(2,1)} %shard_map.112.own), channel_id=1, source_target_pairs={{0,256},{256,0},{128,384},{384,128},{1,257},{257,1},{129,385},{385... | collective-permute-start | bytes 3538952 | tf_op jit(solution)/shard_map/ppermute | solution.py:154
  14.2 129.3 %all-to-all-start = ((bf16[128,8,2048]{2,1,0:T(8,128)(2,1)}), bf16[128,8,2048]{2,1,0:T(8,128)(2,1)}, u32[]{:S(2)}, u32[]{:S(2)}) async-start(bf16[128,8,2048]{2,1,0:T(8,128)(2,1)} %bitcast.18), calls=%async_computation | async-start | bytes 8388608 | tf_op jit(solution)/shard_map/all_to_all | solution.py:385
  35.5 12.3 %collective-permute-start.1 = (bf16[2,3,512,384]{3,2,1,0:T(8,128)(2,1)S(1)}, bf16[2,3,512,384]{3,2,1,0:T(8,128)(2,1)}, u32[]{:S(2)}, u32[]{:S(2)}) collective-permute-start(bf16[2,3,512,384]{3,2,1,0:T(8,128)(2,1)S(1)} %shard_map.113.mine), channel_id=1, source_target_pairs={{0,128},{128,0},{256,384},{384,256},{1,129},{129,1},{257,385},{385... | collective-permute-start | bytes 7077896 | tf_op jit(solution)/shard_map/ppermute | solution.py:156
  50.7 1.8 copy-start.4
  52.5 1.6 copy-start.5
  54.1 1.1 copy-start.6
  158.1 100.1 %all-to-all-start.1 = ((bf16[128,8,1024]{2,1,0:T(8,128)(2,1)}), bf16[128,8,1024]{2,1,0:T(8,128)(2,1)S(1)}, u32[]{:S(2)}, u32[]{:S(2)}) async-start(bf16[128,8,1024]{2,1,0:T(8,128)(2,1)} %bitcast.19), calls=%async_computation.1 | async-start | bytes 4194304 | tf_op jit(solution)/shard_map/all_to_all | solution.py:385
  187.6 9.3 %collective-permute-start.2 = (bf16[2,3,384,512]{3,2,1,0:T(8,128)(2,1)}, bf16[2,3,384,512]{3,2,1,0:T(8,128)(2,1)S(1)}, u32[]{:S(2)}, u32[]{:S(2)}) collective-permute-start(bf16[2,3,384,512]{3,2,1,0:T(8,128)(2,1)} %get-tuple-element.32), channel_id=1, source_target_pairs={{0,128},{128,0},{256,384},{384,256},{1,129},{129,1},{257,385},{385... | collective-permute-start | bytes 7077896 | tf_op jit(solution)/shard_map/ppermute | solution.py:341
  196.9 1.7 copy-start
  199.1 40.0 %collective-permute-start.4 = (bf16[2,384,512]{2,1,0:T(8,128)(2,1)S(1)}, bf16[2,384,512]{2,1,0:T(8,128)(2,1)S(1)}, u32[]{:S(2)}, u32[]{:S(2)}) collective-permute-start(bf16[2,384,512]{2,1,0:T(8,128)(2,1)S(1)} %get-tuple-element.37.sent), channel_id=1, source_target_pairs={{0,256},{256,0},{128,384},{384,128},{1,257},{257,1},{129,385},{385... | collective-permute-start | bytes 2359304 | tf_op jit(solution)/shard_map/ppermute | solution.py:345
  201.0 54.9 %collective-permute-start.3 = (bf16[2,384,512]{2,1,0:T(8,128)(2,1)S(1)}, bf16[2,384,512]{2,1,0:T(8,128)(2,1)S(1)}, u32[]{:S(2)}, u32[]{:S(2)}) collective-permute-start(bf16[2,384,512]{2,1,0:T(8,128)(2,1)S(1)} %get-tuple-element.34), channel_id=1, source_target_pairs={{0,256},{256,0},{128,384},{384,128},{1,257},{257,1},{129,385},{385... | collective-permute-start | bytes 2359304 | tf_op jit(solution)/shard_map/ppermute | solution.py:346
  239.3 17.7 %collective-permute-start.5 = (bf16[2,384,512]{2,1,0:T(8,128)(2,1)S(1)}, bf16[2,384,512]{2,1,0:T(8,128)(2,1)S(1)}, u32[]{:S(2)}, u32[]{:S(2)}) collective-permute-start(bf16[2,384,512]{2,1,0:T(8,128)(2,1)S(1)} %shard_map.121.even), channel_id=1, source_target_pairs={{0,128},{128,0},{256,384},{384,256},{1,129},{129,1},{257,385},{385... | collective-permute-start | bytes 2359304 | tf_op jit(solution)/shard_map/ppermute | solution.py:348
  256.0 2.3 copy-start.7

commit v3 on v2

--- a/solution.py
+++ b/solution.py
@@ -30,6 +30,10 @@
     return jnp.dot(a, b, preferred_element_type=F32)
 
 
+def dot_turned(a, b):
+    return lax.dot_general(a, b, (((1,), (1,)), ((), ())), preferred_element_type=F32)
+
+
 def add(a, b):
     return a.astype(F32) + b.astype(F32)
 
@@ -54,15 +58,22 @@
     return jax.ShapeDtypeStruct(shape, dtype)
 
 
-def local(kernel, outs, *args, scalars=0, moved=4 << 20, flops=0):
+def local(kernel, outs, *args, scalars=0, moved=4 << 20, flops=0, limit=SMALL):
     return pl.pallas_call(
         kernel,
         in_specs=[smem()] * scalars + [vmem()] * (len(args) - scalars),
         out_specs=[vmem()] * len(outs),
         out_shape=outs,
-        compiler_params=pltpu.CompilerParams(vmem_limit_bytes=SMALL),
+        compiler_params=pltpu.CompilerParams(vmem_limit_bytes=limit),
         cost_estimate=cost(flops, moved),
     )(*args)
+
+
+ORDER = (4, 6, 0, 3, 5, 2, 1)
+
+
+def chunk_of(expert):
+    return sum(((expert >> bit) & 1) << k for k, bit in enumerate(ORDER))
 
 
 def send_kernel(experts, cap, ids_ref, weight_ref, scale_ref, codes_ref, grad_ref, send_ref, row_ref, table, place):
@@ -79,8 +90,8 @@
         count = dot(as_bf16(first | second), earlier)
         rank0 = jnp.sum(jnp.where(first, count, 0.0), axis=0, keepdims=True)
         rank1 = jnp.sum(jnp.where(second, count, 0.0), axis=0, keepdims=True)
-        row0 = 2 * cap * ids[0:1, :] + rank0.astype(I32)
-        row1 = 2 * cap * ids[1:2, :] + rank1.astype(I32)
+        row0 = 2 * cap * chunk_of(ids[0:1, :]) + rank0.astype(I32)
+        row1 = 2 * cap * chunk_of(ids[1:2, :]) + rank1.astype(I32)
         place[0:1, :] = row0
         place[1:2, :] = row1
         both = jnp.concatenate([row0.astype(F32), row1.astype(F32), jnp.zeros((tokens - 2, tokens), F32)], axis=0)
@@ -137,27 +148,25 @@
     out[1] = chip[...]
 
 
-def arrange_kernel(dp_ref, mine, theirs, pre_mat, down_mat, back_mat):
+def arrange_kernel(dp_ref, mine, theirs, pre_mat, down_mat):
     width, hid = mine.shape[2:]
     for r, ref in enumerate((mine, theirs, mine, theirs)):
         at = pl.ds(pl.multiple_of((dp_ref[0] ^ r) * width, width), width)
         for k in range(2):
-            value = ref[r // 2, k]
-            pre_mat[at, k * hid : (k + 1) * hid] = value
-            back_mat[k * hid : (k + 1) * hid, at] = value.T
+            pre_mat[at, k * hid : (k + 1) * hid] = ref[r // 2, k]
         down_mat[at, :] = ref[r // 2, 2]
 
 
 def expert_weights(gate, up, down, dp):
     width, hid = gate.shape
-    (own,) = local(pack_kernel, [shaped(3, width, hid)], gate, up, down)
+    (own,) = local(pack_kernel, [shaped(3, width, hid)], gate, up, down, limit=VMEM)
     chip = lax.ppermute(own, "dp", OTHER_CHIP)
     (mine,) = local(merge_kernel, [shaped(2, 3, width, hid)], own, chip, flops=1 << 38)
     theirs = lax.ppermute(mine, "dp", OTHER_CORE)
     full = 4 * width
     return local(
         arrange_kernel,
-        [shaped(full, 2 * hid), shaped(full, hid), shaped(2 * hid, full)],
+        [shaped(full, 2 * hid), shaped(full, hid)],
         dp,
         mine,
         theirs,
@@ -182,7 +191,11 @@
 
 
 def expert_kernel(
-    cap, recv, pre_mat, down_mat, back_mat, back, x_out, dy_out, d_gu, hidden, landed, x, dy, pre, d_hid, dx, recv_sem, out_sem
+    cap,
+    recv, pre_hbm, down_hbm,
+    back_out, d_gu_out, hidden_out,
+    landed, pre_mat, down_mat, x, dy, pre, d_hid, d_gu, hidden, dx, back,
+    recv_sem, mat_sem, out_sem, back_sem,
 ):
     slots, features = x.shape
     hid = hidden.shape[1]
@@ -193,7 +206,18 @@
     arrivals = [
         pltpu.make_async_copy(recv.at[pl.ds(b * block, block)], landed.at[b], recv_sem.at[b]) for b in range(blocks)
     ]
-    for copy in arrivals:
+    mats = [
+        pltpu.make_async_copy(src, dst, mat_sem.at[k])
+        for k, (src, dst) in enumerate(((pre_hbm, pre_mat), (down_hbm, down_mat)))
+    ]
+    leaving = [
+        pltpu.make_async_copy(src, dst, out_sem.at[k])
+        for k, (src, dst) in enumerate(((d_gu, d_gu_out), (hidden, hidden_out)))
+    ]
+    returning = [
+        pltpu.make_async_copy(back.at[b], back_out.at[pl.ds(b * block, block)], back_sem.at[b]) for b in range(blocks)
+    ]
+    for copy in arrivals + mats:
         copy.start()
     gather = gather_matrix(cap, block)
     for b in range(blocks):
@@ -204,11 +228,11 @@
             rows = dot(gather, landed[b, :, part]).astype(BF16)
             x[at, part] = rows[:half]
             dy[at, part] = rows[half:]
-    departures = [pltpu.make_async_copy(x, x_out, out_sem.at[0]), pltpu.make_async_copy(dy, dy_out, out_sem.at[1])]
-    for copy in departures:
-        copy.start()
-
-    pre[...] = dot(x[...], pre_mat[...])
+    mats[0].wait()
+    wide = 256
+    for m in range(0, slots, wide):
+        pre[m : m + wide] = dot(x[m : m + wide], pre_mat[...])
+    mats[1].wait()
     d_hid[...] = dot(dy[...], down_mat[...])
 
     step = 64
@@ -223,52 +247,59 @@
         d_gu[at, 0:hid] = (dh * pu * sig * (1.0 + pg * (1.0 - sig))).astype(BF16)
         d_gu[at, hid : 2 * hid] = (dh * act).astype(BF16)
 
+    for copy in leaving:
+        copy.start()
     for start in range(0, features, width):
         part = slice(start, start + width)
-        dx[:, part] = dot(d_gu[...], back_mat[:, part]).astype(BF16)
+        dx[:, part] = dot_turned(d_gu[...], pre_mat[part, :]).astype(BF16)
     spread = spread_matrix(cap, block)
     for b in range(blocks):
         at = slice(b * half, (b + 1) * half)
         for start in range(0, features // 2, width):
             low, high = slice(start, start + width), slice(features // 2 + start, features // 2 + start + width)
             rows = jnp.concatenate([dx[at, low], dx[at, high]], axis=0)
-            back[b * block : (b + 1) * block, low] = dot(spread, rows).astype(BF16)
-    for copy in departures:
+            back[b, :, low] = dot(spread, rows).astype(BF16)
+        returning[b].start()
+    for copy in leaving + returning:
         copy.wait()
 
 
-def expert_rows(recv, pre_mat, down_mat, back_mat, cap):
+def expert_rows(recv, pre_mat, down_mat, cap):
     total, features = recv.shape
     slots = total // 2
     hid = down_mat.shape[1]
     block = 256
+    blocks = total // block
+    outs = [(total, features // 2), (slots, 2 * hid), (slots, hid)]
+    dma = pltpu.SemaphoreType.DMA
     return pl.pallas_call(
         functools.partial(expert_kernel, cap),
-        in_specs=[anywhere()] + [vmem()] * 3,
-        out_specs=[vmem()] + [anywhere()] * 2 + [vmem()] * 2,
-        out_shape=[
-            shaped(total, features // 2),
-            shaped(slots, features),
-            shaped(slots, features),
-            shaped(slots, 2 * hid),
-            shaped(slots, hid),
-        ],
+        in_specs=[anywhere()] * 3,
+        out_specs=[anywhere()] * 3,
+        out_shape=[shaped(*shape) for shape in outs],
         scratch_shapes=[
-            pltpu.VMEM((total // block, block, features), BF16),
+            pltpu.VMEM((blocks, block, features), BF16),
+            pltpu.VMEM(pre_mat.shape, BF16),
+            pltpu.VMEM(down_mat.shape, BF16),
             pltpu.VMEM((slots, features), BF16),
             pltpu.VMEM((slots, features), BF16),
             pltpu.VMEM((slots, 2 * hid), F32),
             pltpu.VMEM((slots, hid), F32),
+            pltpu.VMEM((slots, 2 * hid), BF16),
+            pltpu.VMEM((slots, hid), BF16),
             pltpu.VMEM((slots, features), BF16),
-            pltpu.SemaphoreType.DMA((total // block,)),
-            pltpu.SemaphoreType.DMA((2,)),
+            pltpu.VMEM((blocks, block, features // 2), BF16),
+            dma((blocks,)),
+            dma((2,)),
+            dma((2,)),
+            dma((blocks,)),
         ],
         compiler_params=pltpu.CompilerParams(vmem_limit_bytes=VMEM),
         cost_estimate=cost(2 * slots * features * hid * 5, 16 << 20, slots * hid),
-    )(recv, pre_mat, down_mat, back_mat)
-
-
-def odd_kernel(dp_ref, x, dy, d_gu, hidden, out, turned_out, turned):
+    )(recv, pre_mat, down_mat)
+
+
+def odd_kernel(cap, dp_ref, recv, d_gu, hidden, out, turned_out, turned, x, dy):
     @pl.when(pl.program_id(0) == 0)
     def _():
         wide = d_gu.shape[1]
@@ -276,34 +307,41 @@
         turned[wide:, :] = hidden[...].T
         turned_out[...] = turned[...]
 
-    even_kernel(dp_ref, x, dy, turned, out)
-
-
-def even_kernel(dp_ref, x, dy, turned, out):
+    even_kernel(cap, dp_ref, recv, turned, out, x, dy)
+
+
+def even_kernel(cap, dp_ref, recv, turned, out, x, dy):
     hid = out.shape[1]
+    block = 256
+    half = block // 2
+    gather = gather_matrix(cap, block)
+    for b in range(recv.shape[0] // block):
+        rows = dot(gather, recv[b * block : (b + 1) * block, :]).astype(BF16)
+        at = slice(b * half, (b + 1) * half)
+        x[at, :] = rows[:half]
+        dy[at, :] = rows[half:]
     for k, rows in enumerate((x, x, dy)):
         out[k] = dot(turned[k * hid : (k + 1) * hid, :], rows[...]).astype(BF16)
 
 
-def partial_grads(kernel, first, dp, x, dy, grads, outs, scratch):
-    slots, features = x.shape
+def partial_grads(kernel, first, dp, recv, grads, outs, scratch, cap):
+    total, features = recv.shape
     width = features // 4
-    rows = pl.BlockSpec((slots, width), lambda i, dp: (0, dp[0] ^ (2 * i + first)))
     whole = lambda a: pl.BlockSpec(a.shape, lambda i, dp: (0, 0))
     hid = outs[0].shape[2]
     return pl.pallas_call(
-        kernel,
+        functools.partial(kernel, cap),
         grid_spec=pltpu.PrefetchScalarGridSpec(
             num_scalar_prefetch=1,
             grid=(2,),
-            in_specs=[rows, rows] + [whole(g) for g in grads],
+            in_specs=[pl.BlockSpec((total, width), lambda i, dp: (0, dp[0] ^ (2 * i + first)))] + [whole(g) for g in grads],
             out_specs=[pl.BlockSpec((None, 3, hid, width), lambda i, dp: (i, 0, 0, 0))] + [whole(o) for o in outs[1:]],
-            scratch_shapes=scratch,
+            scratch_shapes=scratch + [pltpu.VMEM((total // 2, width), BF16)] * 2,
         ),
         out_shape=outs,
         compiler_params=pltpu.CompilerParams(vmem_limit_bytes=VMEM),
-        cost_estimate=cost(12 * slots * width * hid, 6 << 20),
-    )(dp, x, dy, *grads)
+        cost_estimate=cost(6 * total * width * hid, 6 << 20),
+    )(dp, recv, *grads)
 
 
 def first_kernel(even, given, down, gate_up, keep):
@@ -330,16 +368,17 @@
         out[:, pl.ds(pl.multiple_of((dp_ref[0] ^ r) * width, width), width)] = ref[r // 2]
 
 
-def summed_grads(x, dy, d_gu, hidden, dp):
-    slots, features = x.shape
-    width, hid = features // 4, hidden.shape[1]
+def summed_grads(recv, d_gu, hidden, dp, grad_input, cap):
+    features = recv.shape[1]
+    slots, hid = hidden.shape
+    width = features // 4
     part = shaped(2, 3, hid, width)
     turned = shaped(3 * hid, slots)
     odd, grads = partial_grads(
-        odd_kernel, 1, dp, x, dy, (d_gu, hidden), [part, turned], [pltpu.VMEM(turned.shape, BF16)]
+        odd_kernel, 1, dp, recv, (d_gu, hidden), [part, turned], [pltpu.VMEM(turned.shape, BF16)], cap
     )
     given = lax.ppermute(odd, "dp", OTHER_CORE)
-    (even,) = partial_grads(even_kernel, 0, dp, x, dy, (grads,), [part], [])
+    (even,) = partial_grads(even_kernel, 0, dp, recv, (grads,), [part], [], cap)
     two = shaped(2, hid, width)
     down, gate_up, keep = local(first_kernel, [two] * 3, even, given)
     down_other = lax.ppermute(down, "dp", OTHER_CHIP)
@@ -348,7 +387,7 @@
     theirs = lax.ppermute(mine, "dp", OTHER_CORE)
     (grad_down,) = local(place_kernel, [shaped(hid, features)], dp, mine, theirs, scalars=1)
     grad_gate, grad_up = local(gate_up_kernel, [shaped(width, hid)] * 2, keep, gate_up_other)
-    return grad_gate, grad_up, grad_down
+    return grad_input, grad_gate, grad_up, grad_down
 
 
 def token_kernel(cap, row_ref, recv_ref, out_ref):
@@ -378,8 +417,9 @@
 
 def exchange(rows, experts):
     near = experts // 2
+    order = sorted(range(experts), key=chunk_of)
     members = [
-        [(2 * (chip ^ (e // near)) + core) * experts + e for e in range(experts)] for chip in range(2) for core in range(2)
+        [(2 * (chip ^ (e // near)) + core) * experts + e for e in order] for chip in range(2) for core in range(2)
     ]
     chunks = rows.reshape(experts, rows.shape[0] // experts, rows.shape[1])
     moved = lax.all_to_all(chunks, AXES, split_axis=0, concat_axis=0, axis_index_groups=members, tiled=True)
@@ -394,10 +434,10 @@
     mats = expert_weights(w_gate[0], w_up[0], w_down[0], dp)
     send, row_of = rows_to_send(expert_ids.T, route_weight.T, scales.T, codes, grad_out, experts, cap)
     recv = exchange(send, experts)
-    back, x, dy, d_gu, hidden = expert_rows(recv, *mats, cap)
+    back, d_gu, hidden = expert_rows(recv, *mats, cap)
     returned = exchange(back, experts)
-    grad_gate, grad_up, grad_down = summed_grads(x, dy, d_gu, hidden, dp)
     grad_input = token_rows(row_of, returned, tokens, features, cap)
+    grad_input, grad_gate, grad_up, grad_down = summed_grads(recv, d_gu, hidden, dp, grad_input, cap)
     return grad_input, grad_gate[None], grad_up[None], grad_down[None]
 
 

time: 263 us -> 245 us (0.932)
  the two profiles are of different devices: /device:TPU:1 before, /device:TPU:263 now
where the time goes in v3:
time: 245 us
  waiting for transfers between devices  140 us (57%)
  starting transfers between devices  63.8 us (26%)
  Pallas kernels  36.3 us (15%)
  local copies, waits for them, and re-layouts  4.51 us (2%)
    all_to_all x2, waiting for transfers between devices, exchange(): lax.all_to_all(chunks, AXES, split_axis=0, concat_axis=0, axis_index_grou...  74.1 us
    all_to_all x2, starting transfers between devices, exchange(): lax.all_to_all(chunks, AXES, split_axis=0, concat_axis=0, axis_index_grou...  41.6 us
    ppermute x1, waiting for transfers between devices, summed_grads(): down_other = lax.ppermute(down, 'dp', OTHER_CHIP)  37.4 us
    ppermute x1, waiting for transfers between devices, summed_grads(): gate_up_other = lax.ppermute(gate_up, 'dp', OTHER_CHIP)  13.9 us
    pallas_call x1, Pallas kernels, expert_rows(): pl.pallas_call(functools.partial(expert_kernel, cap), in_specs=[anywhere(...  10.4 us
    pallas_call x2, Pallas kernels, partial_grads(): pl.pallas_call(functools.partial(kernel, cap), grid_spec=pltpu.PrefetchSc...  9.99 us
    ppermute x1, waiting for transfers between devices, expert_weights(): chip = lax.ppermute(own, 'dp', OTHER_CHIP)  9.88 us
    pallas_call x7, Pallas kernels, local(): pl.pallas_call(kernel, in_specs=[smem()] * scalars + [vmem()] * (len(args...  8.98 us
  transfers between devices with their start and end apart: 8, of which 5 were waited for; matrix products, arithmetic and copies ran while one was open for 0% of the time, Pallas kernels for 9%

profile of v3, /device:TPU:263, one launch (start us, length us, event | category | flops | bytes accessed | tf_op | source)
XLA Modules:
  0.0 244.9 jit_solution(3544804590241161122)
XLA Ops:
  0.6 2.4 shard_map.112.own
  3.1 3.2 %collective-permute-start = (bf16[3,512,384]{2,1,0:T(8,128)(2,1)}, bf16[3,512,384]{2,1,0:T(8,128)(2,1)}, u32[]{:S(2)}, u32[]{:S(2)}) collective-permute-start(bf16[3,512,384]{2,1,0:T(8,128)(2,1)} %shard_map.112.own), channel_id=1, source_target_pairs={{0,256},{256,0},{128,384},{384,128},{1,257},{257,1},{129,385},{385... | collective-permute-start | bytes 3538952 | tf_op jit(solution)/shard_map/ppermute | solution.py:163
  6.3 5.3 %shard_map.111 = (bf16[1024,2048]{1,0:T(8,128)(2,1)}, s32[128,128]{1,0:T(8,128)}) custom-call(s32[2,128]{1,0:T(2,128)} %bitcast.24, f32[2,128]{1,0:T(2,128)} %bitcast.25, f32[16,128]{1,0:T(8,128)} %bitcast.23, bf16[128,2048]{1,0:T(8,128)(2,1)} %codes_ref.1, bf16[128,2048]{1,0:T(8,128)(2,1)} %grad_ref.1), custom_call_target="tpu_custom_call" | custom-call | flops 274877906944 | bytes 6291456 | tf_op jit(solution)/shard_map/pallas_call | solution.py:128
  11.6 15.6 %all-to-all-start = ((bf16[128,8,2048]{2,1,0:T(8,128)(2,1)}), bf16[128,8,2048]{2,1,0:T(8,128)(2,1)}, u32[]{:S(2)}, u32[]{:S(2)}) async-start(bf16[128,8,2048]{2,1,0:T(8,128)(2,1)} %bitcast.15), calls=%async_computation | async-start | bytes 8388608 | tf_op jit(solution)/shard_map/all_to_all | solution.py:425
  27.1 9.9 %collective-permute-done.chip = bf16[3,512,384]{2,1,0:T(8,128)(2,1)} collective-permute-done((bf16[3,512,384]{2,1,0:T(8,128)(2,1)}, bf16[3,512,384]{2,1,0:T(8,128)(2,1)}, u32[]{:S(2)}, u32[]{:S(2)}) %collective-permute-start) | collective-permute-done | bytes 1179680 | tf_op jit(solution)/shard_map/ppermute | solution.py:163
  37.0 1.5 shard_map.113.mine
  38.5 5.3 %collective-permute-start.1 = (bf16[2,3,512,384]{3,2,1,0:T(8,128)(2,1)S(1)}, bf16[2,3,512,384]{3,2,1,0:T(8,128)(2,1)}, u32[]{:S(2)}, u32[]{:S(2)}) collective-permute-start(bf16[2,3,512,384]{3,2,1,0:T(8,128)(2,1)S(1)} %shard_map.113.mine), channel_id=1, source_target_pairs={{0,128},{128,0},{256,384},{384,256},{1,129},{129,1},{257,385},{385... | collective-permute-start | bytes 7077896 | tf_op jit(solution)/shard_map/ppermute | solution.py:165
  43.8 4.3 %collective-permute-done.1.theirs = bf16[2,3,512,384]{3,2,1,0:T(8,128)(2,1)} collective-permute-done((bf16[2,3,512,384]{3,2,1,0:T(8,128)(2,1)S(1)}, bf16[2,3,512,384]{3,2,1,0:T(8,128)(2,1)}, u32[]{:S(2)}, u32[]{:S(2)}) %collective-permute-start.1) | collective-permute-done | bytes 2359328 | tf_op jit(solution)/shard_map/ppermute | solution.py:165
  48.1 2.1 shard_map.114
  50.2 1.7 copy-done.2
  53.0 74.1 %all-to-all-done = bf16[128,8,2048]{2,1,0:T(8,128)(2,1)} async-done(((bf16[128,8,2048]{2,1,0:T(8,128)(2,1)}), bf16[128,8,2048]{2,1,0:T(8,128)(2,1)}, u32[]{:S(2)}, u32[]{:S(2)}) %all-to-all-start) | async-done | bytes 4194336 | tf_op jit(solution)/shard_map/all_to_all | solution.py:425
  127.1 10.4 %shard_map.115 = (bf16[1024,1024]{1,0:T(8,128)(2,1)}, bf16[512,768]{1,0:T(8,128)(2,1)}, bf16[512,384]{1,0:T(8,128)(2,1)}) custom-call(bf16[1024,2048]{1,0:T(8,128)(2,1)} %bitcast.4.recv, bf16[2048,768]{1,0:T(8,128)(2,1)} %copy-done.2, bf16[2048,384]{1,0:T(8,128)(2,1)} %copy-done.3), custom_call_target="tpu_custom_call" | custom-call | flops 4026531840 | bytes 16777216 | tf_op jit(solution)/shard_map/pallas_call | solution.py:275
  137.6 26.0 %all-to-all-start.1 = ((bf16[128,8,1024]{2,1,0:T(8,128)(2,1)}), bf16[128,8,1024]{2,1,0:T(8,128)(2,1)S(1)}, u32[]{:S(2)}, u32[]{:S(2)}) async-start(bf16[128,8,1024]{2,1,0:T(8,128)(2,1)} %bitcast.16), calls=%async_computation.1 | async-start | bytes 4194304 | tf_op jit(solution)/shard_map/all_to_all | solution.py:425
  163.6 5.2 %shard_map.117 = (bf16[2,3,384,512]{3,2,1,0:T(8,128)(2,1)}, bf16[1152,512]{1,0:T(8,128)(2,1)}) custom-call(s32[1]{0:T(128)} %bitcast.5.dp_ref, bf16[1024,2048]{1,0:T(8,128)(2,1)} %bitcast.4.recv, bf16[512,768]{1,0:T(8,128)(2,1)} %get-tuple-element.23.d_gu, bf16[512,384]{1,0:T(8,128)(2,1)} %get-tuple-element.24.hidden), custom_call_target="tpu_custom_call" | custom-call | flops 1207959552 | bytes 6291456 | tf_op jit(solution)/shard_map/pallas_call | solution.py:332
  168.8 5.6 %collective-permute-start.2 = (bf16[2,3,384,512]{3,2,1,0:T(8,128)(2,1)}, bf16[2,3,384,512]{3,2,1,0:T(8,128)(2,1)S(1)}, u32[]{:S(2)}, u32[]{:S(2)}) collective-permute-start(bf16[2,3,384,512]{3,2,1,0:T(8,128)(2,1)} %get-tuple-element.26), channel_id=1, source_target_pairs={{0,128},{128,0},{256,384},{384,256},{1,129},{129,1},{257,385},{385... | collective-permute-start | bytes 7077896 | tf_op jit(solution)/shard_map/ppermute | solution.py:380
  174.5 4.8 %shard_map.118.even = bf16[2,3,384,512]{3,2,1,0:T(8,128)(2,1)} custom-call(s32[1]{0:T(128)} %bitcast.5.dp_ref, bf16[1024,2048]{1,0:T(8,128)(2,1)} %bitcast.4.recv, bf16[1152,512]{1,0:T(8,128)(2,1)} %get-tuple-element.25.turned), custom_call_target="tpu_custom_call" | custom-call | flops 1207959552 | bytes 6291456 | tf_op jit(solution)/shard_map/pallas_call | solution.py:332
  179.2 1.7 copy-done
  181.4 1.9 collective-permute-start.4
  183.4 3.4 %collective-permute-start.3 = (bf16[2,384,512]{2,1,0:T(8,128)(2,1)S(1)}, bf16[2,384,512]{2,1,0:T(8,128)(2,1)S(1)}, u32[]{:S(2)}, u32[]{:S(2)}) collective-permute-start(bf16[2,384,512]{2,1,0:T(8,128)(2,1)S(1)} %get-tuple-element.28), channel_id=1, source_target_pairs={{0,256},{256,0},{128,384},{384,128},{1,257},{257,1},{129,385},{385... | collective-permute-start | bytes 2359304 | tf_op jit(solution)/shard_map/ppermute | solution.py:385
  186.7 37.4 %collective-permute-done.4.other = bf16[2,384,512]{2,1,0:T(8,128)(2,1)S(1)} collective-permute-done((bf16[2,384,512]{2,1,0:T(8,128)(2,1)S(1)}, bf16[2,384,512]{2,1,0:T(8,128)(2,1)S(1)}, u32[]{:S(2)}, u32[]{:S(2)}) %collective-permute-start.4) | collective-permute-done | bytes 786464 | tf_op jit(solution)/shard_map/ppermute | solution.py:384
  224.3 2.8 %collective-permute-start.5 = (bf16[2,384,512]{2,1,0:T(8,128)(2,1)S(1)}, bf16[2,384,512]{2,1,0:T(8,128)(2,1)S(1)}, u32[]{:S(2)}, u32[]{:S(2)}) collective-permute-start(bf16[2,384,512]{2,1,0:T(8,128)(2,1)S(1)} %shard_map.121.even), channel_id=1, source_target_pairs={{0,128},{128,0},{256,384},{384,256},{1,129},{129,1},{257,385},{385... | collective-permute-start | bytes 2359304 | tf_op jit(solution)/shard_map/ppermute | solution.py:387
  227.0 13.9 %collective-permute-done.3.other = bf16[2,384,512]{2,1,0:T(8,128)(2,1)S(1)} collective-permute-done((bf16[2,384,512]{2,1,0:T(8,128)(2,1)S(1)}, bf16[2,384,512]{2,1,0:T(8,128)(2,1)S(1)}, u32[]{:S(2)}, u32[]{:S(2)}) %collective-permute-start.3) | collective-permute-done | bytes 786464 | tf_op jit(solution)/shard_map/ppermute | solution.py:385
  242.0 1.3 shard_map.122
  243.3 1.6 shard_map.116
  (14 shorter events, 2.9 us)
Async XLA Ops:
  3.1 34.0 %collective-permute-start = (bf16[3,512,384]{2,1,0:T(8,128)(2,1)}, bf16[3,512,384]{2,1,0:T(8,128)(2,1)}, u32[]{:S(2)}, u32[]{:S(2)}) collective-permute-start(bf16[3,512,384]{2,1,0:T(8,128)(2,1)} %shard_map.112.own), channel_id=1, source_target_pairs={{0,256},{256,0},{128,384},{384,128},{1,257},{257,1},{129,385},{385... | collective-permute-start | bytes 3538952 | tf_op jit(solution)/shard_map/ppermute | solution.py:163
  11.5 25.5 %copy-start.1 = (bf16[3,512,384]{2,1,0:T(8,128)(2,1)S(1)}, bf16[3,512,384]{2,1,0:T(8,128)(2,1)}, u32[]{:S(2)}) copy-start(bf16[3,512,384]{2,1,0:T(8,128)(2,1)} %shard_map.112.own) | copy-start | bytes 3538948
  11.6 115.6 %all-to-all-start = ((bf16[128,8,2048]{2,1,0:T(8,128)(2,1)}), bf16[128,8,2048]{2,1,0:T(8,128)(2,1)}, u32[]{:S(2)}, u32[]{:S(2)}) async-start(bf16[128,8,2048]{2,1,0:T(8,128)(2,1)} %bitcast.15), calls=%async_computation | async-start | bytes 8388608 | tf_op jit(solution)/shard_map/all_to_all | solution.py:425
  38.5 9.6 %collective-permute-start.1 = (bf16[2,3,512,384]{3,2,1,0:T(8,128)(2,1)S(1)}, bf16[2,3,512,384]{3,2,1,0:T(8,128)(2,1)}, u32[]{:S(2)}, u32[]{:S(2)}) collective-permute-start(bf16[2,3,512,384]{3,2,1,0:T(8,128)(2,1)S(1)} %shard_map.113.mine), channel_id=1, source_target_pairs={{0,128},{128,0},{256,384},{384,256},{1,129},{129,1},{257,385},{385... | collective-permute-start | bytes 7077896 | tf_op jit(solution)/shard_map/ppermute | solution.py:165
  50.2 1.7 copy-start.2
  51.9 1.1 copy-start.3
  137.6 105.6 %all-to-all-start.1 = ((bf16[128,8,1024]{2,1,0:T(8,128)(2,1)}), bf16[128,8,1024]{2,1,0:T(8,128)(2,1)S(1)}, u32[]{:S(2)}, u32[]{:S(2)}) async-start(bf16[128,8,1024]{2,1,0:T(8,128)(2,1)} %bitcast.16), calls=%async_computation.1 | async-start | bytes 4194304 | tf_op jit(solution)/shard_map/all_to_all | solution.py:425
  168.8 10.4 %collective-permute-start.2 = (bf16[2,3,384,512]{3,2,1,0:T(8,128)(2,1)}, bf16[2,3,384,512]{3,2,1,0:T(8,128)(2,1)S(1)}, u32[]{:S(2)}, u32[]{:S(2)}) collective-permute-start(bf16[2,3,384,512]{3,2,1,0:T(8,128)(2,1)} %get-tuple-element.26), channel_id=1, source_target_pairs={{0,128},{128,0},{256,384},{384,256},{1,129},{129,1},{257,385},{385... | collective-permute-start | bytes 7077896 | tf_op jit(solution)/shard_map/ppermute | solution.py:380
  179.2 1.7 copy-start
  181.4 42.7 %collective-permute-start.4 = (bf16[2,384,512]{2,1,0:T(8,128)(2,1)S(1)}, bf16[2,384,512]{2,1,0:T(8,128)(2,1)S(1)}, u32[]{:S(2)}, u32[]{:S(2)}) collective-permute-start(bf16[2,384,512]{2,1,0:T(8,128)(2,1)S(1)} %get-tuple-element.31.sent), channel_id=1, source_target_pairs={{0,256},{256,0},{128,384},{384,128},{1,257},{257,1},{129,385},{385... | collective-permute-start | bytes 2359304 | tf_op jit(solution)/shard_map/ppermute | solution.py:384
  183.4 57.6 %collective-permute-start.3 = (bf16[2,384,512]{2,1,0:T(8,128)(2,1)S(1)}, bf16[2,384,512]{2,1,0:T(8,128)(2,1)S(1)}, u32[]{:S(2)}, u32[]{:S(2)}) collective-permute-start(bf16[2,384,512]{2,1,0:T(8,128)(2,1)S(1)} %get-tuple-element.28), channel_id=1, source_target_pairs={{0,256},{256,0},{128,384},{384,128},{1,257},{257,1},{129,385},{385... | collective-permute-start | bytes 2359304 | tf_op jit(solution)/shard_map/ppermute | solution.py:385
  224.3 17.7 %collective-permute-start.5 = (bf16[2,384,512]{2,1,0:T(8,128)(2,1)S(1)}, bf16[2,384,512]{2,1,0:T(8,128)(2,1)S(1)}, u32[]{:S(2)}, u32[]{:S(2)}) collective-permute-start(bf16[2,384,512]{2,1,0:T(8,128)(2,1)S(1)} %shard_map.121.even), channel_id=1, source_target_pairs={{0,128},{128,0},{256,384},{384,256},{1,129},{129,1},{257,385},{385... | collective-permute-start | bytes 2359304 | tf_op jit(solution)/shard_map/ppermute | solution.py:387
  240.9 2.3 copy-start.4

commit v4 on v3

--- a/solution.py
+++ b/solution.py
@@ -76,7 +76,11 @@
     return sum(((expert >> bit) & 1) << k for k, bit in enumerate(ORDER))
 
 
-def send_kernel(experts, cap, ids_ref, weight_ref, scale_ref, codes_ref, grad_ref, send_ref, row_ref, table, place):
+def send_kernel(
+    experts, cap,
+    ids_ref, weight_ref, scale_ref, codes_ref, grad_ref, gate, up, down,
+    send_ref, row_ref, own_ref, table, place,
+):
     step = pl.program_id(0)
     tokens, features = codes_ref.shape
     rows = send_ref.shape[0]
@@ -104,6 +108,12 @@
             table[0:tokens, part] = (codes_ref[:, part].astype(F32) * scale[:, j : j + 1]).astype(BF16)
         table[tokens : 2 * tokens, :] = grad_ref[...]
 
+    @pl.when(step == pl.num_programs(0) - 1)
+    def _():
+        own_ref[0] = gate[...]
+        own_ref[1] = up[...]
+        own_ref[2] = down[...].T
+
     row = iota((rows, tokens), 0) + step * rows
     is_grad = (row & cap) != 0
     base = row - (row & cap)
@@ -120,27 +130,27 @@
         send_ref[:, part] = (dot(pick, table[:, part]) * weight).astype(BF16)
 
 
-def rows_to_send(ids, weights, scales, codes, grads, experts, cap):
+def rows_to_send(ids, weights, scales, codes, grads, gate, up, down, experts, cap):
     tokens, features = codes.shape
     total = 2 * experts * cap
-    rows = 256
+    rows = 512
     whole = lambda a: pl.BlockSpec(a.shape, lambda i: (0, 0))
+    own = shaped(3, *gate.shape)
+    args = (ids, weights, scales, codes, grads, gate, up, down)
     return pl.pallas_call(
         functools.partial(send_kernel, experts, cap),
         grid=(total // rows,),
-        in_specs=[whole(a) for a in (ids, weights, scales, codes, grads)],
-        out_specs=[pl.BlockSpec((rows, features), lambda i: (i, 0)), pl.BlockSpec((tokens, tokens), lambda i: (0, 0))],
-        out_shape=[shaped(total, features), shaped(tokens, tokens, dtype=I32)],
+        in_specs=[whole(a) for a in args],
+        out_specs=[
+            pl.BlockSpec((rows, features), lambda i: (i, 0)),
+            pl.BlockSpec((tokens, tokens), lambda i: (0, 0)),
+            pl.BlockSpec(own.shape, lambda i: (0, 0, 0)),
+        ],
+        out_shape=[shaped(total, features), shaped(tokens, tokens, dtype=I32), own],
         scratch_shapes=[pltpu.VMEM((2 * tokens, features), BF16), pltpu.VMEM((8, tokens), I32)],
         compiler_params=pltpu.CompilerParams(vmem_limit_bytes=VMEM),
         cost_estimate=cost(1 << 38, 6 << 20),
-    )(ids, weights, scales, codes, grads)
-
-
-def pack_kernel(gate, up, down, out):
-    out[0] = gate[...]
-    out[1] = up[...]
-    out[2] = down[...].T
+    )(*args)
 
 
 def merge_kernel(own, chip, out):
@@ -157,9 +167,8 @@
         down_mat[at, :] = ref[r // 2, 2]
 
 
-def expert_weights(gate, up, down, dp):
-    width, hid = gate.shape
-    (own,) = local(pack_kernel, [shaped(3, width, hid)], gate, up, down, limit=VMEM)
+def expert_weights(own, dp):
+    width, hid = own.shape[1:]
     chip = lax.ppermute(own, "dp", OTHER_CHIP)
     (mine,) = local(merge_kernel, [shaped(2, 3, width, hid)], own, chip, flops=1 << 38)
     theirs = lax.ppermute(mine, "dp", OTHER_CORE)
@@ -431,8 +440,10 @@
     experts = lax.axis_size("expert") * lax.axis_size("seq")
     cap = 2 * tokens * expert_ids.shape[1] // experts
     dp = lax.axis_index("dp").astype(I32).reshape(1)
-    mats = expert_weights(w_gate[0], w_up[0], w_down[0], dp)
-    send, row_of = rows_to_send(expert_ids.T, route_weight.T, scales.T, codes, grad_out, experts, cap)
+    send, row_of, own = rows_to_send(
+        expert_ids.T, route_weight.T, scales.T, codes, grad_out, w_gate[0], w_up[0], w_down[0], experts, cap
+    )
+    mats = expert_weights(own, dp)
     recv = exchange(send, experts)
     back, d_gu, hidden = expert_rows(recv, *mats, cap)
     returned = exchange(back, experts)

time: 245 us -> 242 us (0.988)
  the two profiles are of different devices: /device:TPU:263 before, /device:TPU:1 now
where the time goes in v4:
time: 242 us; the launch traced here: 241 us
  waiting for transfers between devices  118 us (49%)
  starting transfers between devices  82.6 us (34%)
  Pallas kernels  32.7 us (14%)
  local copies, waits for them, and re-layouts  6.87 us (3%)
    all_to_all x2, waiting for transfers between devices, exchange(): lax.all_to_all(chunks, AXES, split_axis=0, concat_axis=0, axis_index_grou...  66.7 us
    all_to_all x2, starting transfers between devices, exchange(): lax.all_to_all(chunks, AXES, split_axis=0, concat_axis=0, axis_index_grou...  39.4 us
    ppermute x1, waiting for transfers between devices, summed_grads(): down_other = lax.ppermute(down, 'dp', OTHER_CHIP)  33.2 us
    ppermute x1, starting transfers between devices, expert_weights(): theirs = lax.ppermute(mine, 'dp', OTHER_CORE)  23.7 us
    ppermute x1, waiting for transfers between devices, summed_grads(): gate_up_other = lax.ppermute(gate_up, 'dp', OTHER_CHIP)  12.2 us
    pallas_call x1, Pallas kernels, expert_rows(): pl.pallas_call(functools.partial(expert_kernel, cap), in_specs=[anywhere(...  10.4 us
    pallas_call x2, Pallas kernels, partial_grads(): pl.pallas_call(functools.partial(kernel, cap), grid_spec=pltpu.PrefetchSc...  9.99 us
    unnamed x14, local copies, waits for them, and re-layouts  6.87 us
  transfers between devices with their start and end apart: 8, of which 5 were waited for; matrix products, arithmetic and copies ran while one was open for 0% of the time, Pallas kernels for 6%

profile of v4, /device:TPU:1, one launch (start us, length us, event | category | flops | bytes accessed | tf_op | source)
XLA Modules:
  0.0 240.8 jit_solution(5873501888733303176)
XLA Ops:
  0.6 5.4 %shard_map.111 = (bf16[1024,2048]{1,0:T(8,128)(2,1)}, s32[128,128]{1,0:T(8,128)}, bf16[3,512,384]{2,1,0:T(8,128)(2,1)}) custom-call(s32[2,128]{1,0:T(2,128)} %bitcast.24, f32[2,128]{1,0:T(2,128)} %bitcast.25, f32[16,128]{1,0:T(8,128)} %bitcast.23, bf16[128,2048]{1,0:T(8,128)(2,1)} %codes_ref.1, bf16[128,2048]{1,0:T(8,128)(2,1)} %grad_ref.1, ...), custom_call_target="tpu_custom_call" | custom-call | flops 274877906944 | bytes 6291456 | tf_op jit(solution)/shard_map/pallas_call | solution.py:140
  6.0 4.0 %collective-permute-start = (bf16[3,512,384]{2,1,0:T(8,128)(2,1)}, bf16[3,512,384]{2,1,0:T(8,128)(2,1)S(1)}, u32[]{:S(2)}, u32[]{:S(2)}) collective-permute-start(bf16[3,512,384]{2,1,0:T(8,128)(2,1)} %get-tuple-element.21.own), channel_id=1, source_target_pairs={{0,256},{256,0},{128,384},{384,128},{1,257},{257,1},{129,385},{385... | collective-permute-start | bytes 3538952 | tf_op jit(solution)/shard_map/ppermute | solution.py:172
  10.1 19.7 %all-to-all-start = ((bf16[128,8,2048]{2,1,0:T(8,128)(2,1)}), bf16[128,8,2048]{2,1,0:T(8,128)(2,1)}, u32[]{:S(2)}, u32[]{:S(2)}) async-start(bf16[128,8,2048]{2,1,0:T(8,128)(2,1)} %bitcast.15), calls=%async_computation | async-start | bytes 8388608 | tf_op jit(solution)/shard_map/all_to_all | solution.py:434
  29.7 1.5 collective-permute-done.chip
  32.3 1.3 copy-done.5
  33.8 23.7 %collective-permute-start.1 = (bf16[2,3,512,384]{3,2,1,0:T(8,128)(2,1)S(1)}, bf16[2,3,512,384]{3,2,1,0:T(8,128)(2,1)}, u32[]{:S(2)}, u32[]{:S(2)}) collective-permute-start(bf16[2,3,512,384]{3,2,1,0:T(8,128)(2,1)S(1)} %shard_map.112.mine), channel_id=1, source_target_pairs={{0,128},{128,0},{256,384},{384,256},{1,129},{129,1},{257,385},{385... | collective-permute-start | bytes 7077896 | tf_op jit(solution)/shard_map/ppermute | solution.py:174
  57.5 4.3 %collective-permute-done.1.theirs = bf16[2,3,512,384]{3,2,1,0:T(8,128)(2,1)} collective-permute-done((bf16[2,3,512,384]{3,2,1,0:T(8,128)(2,1)S(1)}, bf16[2,3,512,384]{3,2,1,0:T(8,128)(2,1)}, u32[]{:S(2)}, u32[]{:S(2)}) %collective-permute-start.1) | collective-permute-done | bytes 2359328 | tf_op jit(solution)/shard_map/ppermute | solution.py:174
  61.8 2.1 shard_map.113
  63.9 1.7 copy-done.1
  65.6 1.1 copy-done.2
  66.7 66.7 %all-to-all-done = bf16[128,8,2048]{2,1,0:T(8,128)(2,1)} async-done(((bf16[128,8,2048]{2,1,0:T(8,128)(2,1)}), bf16[128,8,2048]{2,1,0:T(8,128)(2,1)}, u32[]{:S(2)}, u32[]{:S(2)}) %all-to-all-start) | async-done | bytes 4194336 | tf_op jit(solution)/shard_map/all_to_all | solution.py:434
  133.4 10.4 %shard_map.114 = (bf16[1024,1024]{1,0:T(8,128)(2,1)}, bf16[512,768]{1,0:T(8,128)(2,1)}, bf16[512,384]{1,0:T(8,128)(2,1)}) custom-call(bf16[1024,2048]{1,0:T(8,128)(2,1)} %bitcast.7.recv, bf16[2048,768]{1,0:T(8,128)(2,1)} %copy-done.1, bf16[2048,384]{1,0:T(8,128)(2,1)} %copy-done.2), custom_call_target="tpu_custom_call" | custom-call | flops 4026531840 | bytes 16777216 | tf_op jit(solution)/shard_map/pallas_call | solution.py:284
  143.9 19.8 %all-to-all-start.1 = ((bf16[128,8,1024]{2,1,0:T(8,128)(2,1)}), bf16[128,8,1024]{2,1,0:T(8,128)(2,1)S(1)}, u32[]{:S(2)}, u32[]{:S(2)}) async-start(bf16[128,8,1024]{2,1,0:T(8,128)(2,1)} %bitcast.16), calls=%async_computation.1 | async-start | bytes 4194304 | tf_op jit(solution)/shard_map/all_to_all | solution.py:434
  163.6 5.2 %shard_map.116 = (bf16[2,3,384,512]{3,2,1,0:T(8,128)(2,1)}, bf16[1152,512]{1,0:T(8,128)(2,1)}) custom-call(s32[1]{0:T(128)} %bitcast.8.dp_ref, bf16[1024,2048]{1,0:T(8,128)(2,1)} %bitcast.7.recv, bf16[512,768]{1,0:T(8,128)(2,1)} %get-tuple-element.25.d_gu, bf16[512,384]{1,0:T(8,128)(2,1)} %get-tuple-element.26.hidden), custom_call_target="tpu_custom_call" | custom-call | flops 1207959552 | bytes 6291456 | tf_op jit(solution)/shard_map/pallas_call | solution.py:341
  168.9 5.7 %collective-permute-start.2 = (bf16[2,3,384,512]{3,2,1,0:T(8,128)(2,1)}, bf16[2,3,384,512]{3,2,1,0:T(8,128)(2,1)S(1)}, u32[]{:S(2)}, u32[]{:S(2)}) collective-permute-start(bf16[2,3,384,512]{3,2,1,0:T(8,128)(2,1)} %get-tuple-element.28), channel_id=1, source_target_pairs={{0,128},{128,0},{256,384},{384,256},{1,129},{129,1},{257,385},{385... | collective-permute-start | bytes 7077896 | tf_op jit(solution)/shard_map/ppermute | solution.py:389
  174.6 4.7 %shard_map.117.even = bf16[2,3,384,512]{3,2,1,0:T(8,128)(2,1)} custom-call(s32[1]{0:T(128)} %bitcast.8.dp_ref, bf16[1024,2048]{1,0:T(8,128)(2,1)} %bitcast.7.recv, bf16[1152,512]{1,0:T(8,128)(2,1)} %get-tuple-element.27.turned), custom_call_target="tpu_custom_call" | custom-call | flops 1207959552 | bytes 6291456 | tf_op jit(solution)/shard_map/pallas_call | solution.py:341
  179.3 1.7 copy-done
  181.5 1.9 collective-permute-start.4
  183.5 3.4 %collective-permute-start.3 = (bf16[2,384,512]{2,1,0:T(8,128)(2,1)S(1)}, bf16[2,384,512]{2,1,0:T(8,128)(2,1)S(1)}, u32[]{:S(2)}, u32[]{:S(2)}) collective-permute-start(bf16[2,384,512]{2,1,0:T(8,128)(2,1)S(1)} %get-tuple-element.30), channel_id=1, source_target_pairs={{0,256},{256,0},{128,384},{384,128},{1,257},{257,1},{129,385},{385... | collective-permute-start | bytes 2359304 | tf_op jit(solution)/shard_map/ppermute | solution.py:394
  186.8 33.2 %collective-permute-done.4.other = bf16[2,384,512]{2,1,0:T(8,128)(2,1)S(1)} collective-permute-done((bf16[2,384,512]{2,1,0:T(8,128)(2,1)S(1)}, bf16[2,384,512]{2,1,0:T(8,128)(2,1)S(1)}, u32[]{:S(2)}, u32[]{:S(2)}) %collective-permute-start.4) | collective-permute-done | bytes 786464 | tf_op jit(solution)/shard_map/ppermute | solution.py:393
  220.2 4.5 %collective-permute-start.5 = (bf16[2,384,512]{2,1,0:T(8,128)(2,1)S(1)}, bf16[2,384,512]{2,1,0:T(8,128)(2,1)S(1)}, u32[]{:S(2)}, u32[]{:S(2)}) collective-permute-start(bf16[2,384,512]{2,1,0:T(8,128)(2,1)S(1)} %shard_map.120.even), channel_id=1, source_target_pairs={{0,128},{128,0},{256,384},{384,256},{1,129},{129,1},{257,385},{385... | collective-permute-start | bytes 2359304 | tf_op jit(solution)/shard_map/ppermute | solution.py:396
  224.7 12.2 %collective-permute-done.3.other = bf16[2,384,512]{2,1,0:T(8,128)(2,1)S(1)} collective-permute-done((bf16[2,384,512]{2,1,0:T(8,128)(2,1)S(1)}, bf16[2,384,512]{2,1,0:T(8,128)(2,1)S(1)}, u32[]{:S(2)}, u32[]{:S(2)}) %collective-permute-start.3) | collective-permute-done | bytes 786464 | tf_op jit(solution)/shard_map/ppermute | solution.py:394
  237.9 1.3 shard_map.121
  239.1 1.6 shard_map.115
  (17 shorter events, 3.1 us)
Async XLA Ops:
  6.0 25.2 %collective-permute-start = (bf16[3,512,384]{2,1,0:T(8,128)(2,1)}, bf16[3,512,384]{2,1,0:T(8,128)(2,1)S(1)}, u32[]{:S(2)}, u32[]{:S(2)}) collective-permute-start(bf16[3,512,384]{2,1,0:T(8,128)(2,1)} %get-tuple-element.21.own), channel_id=1, source_target_pairs={{0,256},{256,0},{128,384},{384,128},{1,257},{257,1},{129,385},{385... | collective-permute-start | bytes 3538952 | tf_op jit(solution)/shard_map/ppermute | solution.py:172
  10.1 22.3 %copy-start.3 = (bf16[3,512,384]{2,1,0:T(8,128)(2,1)S(1)}, bf16[3,512,384]{2,1,0:T(8,128)(2,1)}, u32[]{:S(2)}) copy-start(bf16[3,512,384]{2,1,0:T(8,128)(2,1)} %get-tuple-element.21.own) | copy-start | bytes 3538948
  10.1 123.4 %all-to-all-start = ((bf16[128,8,2048]{2,1,0:T(8,128)(2,1)}), bf16[128,8,2048]{2,1,0:T(8,128)(2,1)}, u32[]{:S(2)}, u32[]{:S(2)}) async-start(bf16[128,8,2048]{2,1,0:T(8,128)(2,1)} %bitcast.15), calls=%async_computation | async-start | bytes 8388608 | tf_op jit(solution)/shard_map/all_to_all | solution.py:434
  31.2 1.1 copy-start.4
  32.3 1.3 copy-start.5
  33.8 28.0 %collective-permute-start.1 = (bf16[2,3,512,384]{3,2,1,0:T(8,128)(2,1)S(1)}, bf16[2,3,512,384]{3,2,1,0:T(8,128)(2,1)}, u32[]{:S(2)}, u32[]{:S(2)}) collective-permute-start(bf16[2,3,512,384]{3,2,1,0:T(8,128)(2,1)S(1)} %shard_map.112.mine), channel_id=1, source_target_pairs={{0,128},{128,0},{256,384},{384,256},{1,129},{129,1},{257,385},{385... | collective-permute-start | bytes 7077896 | tf_op jit(solution)/shard_map/ppermute | solution.py:174
  63.9 1.7 copy-start.1
  65.6 1.1 copy-start.2
  143.9 95.3 %all-to-all-start.1 = ((bf16[128,8,1024]{2,1,0:T(8,128)(2,1)}), bf16[128,8,1024]{2,1,0:T(8,128)(2,1)S(1)}, u32[]{:S(2)}, u32[]{:S(2)}) async-start(bf16[128,8,1024]{2,1,0:T(8,128)(2,1)} %bitcast.16), calls=%async_computation.1 | async-start | bytes 4194304 | tf_op jit(solution)/shard_map/all_to_all | solution.py:434
  168.9 10.5 %collective-permute-start.2 = (bf16[2,3,384,512]{3,2,1,0:T(8,128)(2,1)}, bf16[2,3,384,512]{3,2,1,0:T(8,128)(2,1)S(1)}, u32[]{:S(2)}, u32[]{:S(2)}) collective-permute-start(bf16[2,3,384,512]{3,2,1,0:T(8,128)(2,1)} %get-tuple-element.28), channel_id=1, source_target_pairs={{0,128},{128,0},{256,384},{384,256},{1,129},{129,1},{257,385},{385... | collective-permute-start | bytes 7077896 | tf_op jit(solution)/shard_map/ppermute | solution.py:389
  179.3 1.7 copy-start
  181.5 38.5 %collective-permute-start.4 = (bf16[2,384,512]{2,1,0:T(8,128)(2,1)S(1)}, bf16[2,384,512]{2,1,0:T(8,128)(2,1)S(1)}, u32[]{:S(2)}, u32[]{:S(2)}) collective-permute-start(bf16[2,384,512]{2,1,0:T(8,128)(2,1)S(1)} %get-tuple-element.33.sent), channel_id=1, source_target_pairs={{0,256},{256,0},{128,384},{384,128},{1,257},{257,1},{129,385},{385... | collective-permute-start | bytes 2359304 | tf_op jit(solution)/shard_map/ppermute | solution.py:393
  183.5 53.4 %collective-permute-start.3 = (bf16[2,384,512]{2,1,0:T(8,128)(2,1)S(1)}, bf16[2,384,512]{2,1,0:T(8,128)(2,1)S(1)}, u32[]{:S(2)}, u32[]{:S(2)}) collective-permute-start(bf16[2,384,512]{2,1,0:T(8,128)(2,1)S(1)} %get-tuple-element.30), channel_id=1, source_target_pairs={{0,256},{256,0},{128,384},{384,128},{1,257},{257,1},{129,385},{385... | collective-permute-start | bytes 2359304 | tf_op jit(solution)/shard_map/ppermute | solution.py:394
  220.2 17.7 %collective-permute-start.5 = (bf16[2,384,512]{2,1,0:T(8,128)(2,1)S(1)}, bf16[2,384,512]{2,1,0:T(8,128)(2,1)S(1)}, u32[]{:S(2)}, u32[]{:S(2)}) collective-permute-start(bf16[2,384,512]{2,1,0:T(8,128)(2,1)S(1)} %shard_map.120.even), channel_id=1, source_target_pairs={{0,128},{128,0},{256,384},{384,256},{1,129},{129,1},{257,385},{385... | collective-permute-start | bytes 2359304 | tf_op jit(solution)/shard_map/ppermute | solution.py:396
  236.8 2.3 copy-start.6

commit v5 on v4

--- a/solution.py
+++ b/solution.py
@@ -226,7 +226,7 @@
     returning = [
         pltpu.make_async_copy(back.at[b], back_out.at[pl.ds(b * block, block)], back_sem.at[b]) for b in range(blocks)
     ]
-    for copy in arrivals + mats:
+    for copy in arrivals + mats[::-1]:
         copy.start()
     gather = gather_matrix(cap, block)
     for b in range(blocks):
@@ -237,12 +237,12 @@
             rows = dot(gather, landed[b, :, part]).astype(BF16)
             x[at, part] = rows[:half]
             dy[at, part] = rows[half:]
+    mats[1].wait()
+    d_hid[...] = dot(dy[...], down_mat[...])
     mats[0].wait()
     wide = 256
     for m in range(0, slots, wide):
         pre[m : m + wide] = dot(x[m : m + wide], pre_mat[...])
-    mats[1].wait()
-    d_hid[...] = dot(dy[...], down_mat[...])
 
     step = 64
 

time: 242 us -> 242 us (level)
  no operation moved by 1% of the time
where the time goes in v5:
time: 242 us; the launch traced here: 240 us
  waiting for transfers between devices  118 us (49%)
  starting transfers between devices  82.6 us (34%)
  Pallas kernels  32.3 us (13%)
  local copies, waits for them, and re-layouts  6.87 us (3%)
    all_to_all x2, waiting for transfers between devices, exchange(): lax.all_to_all(chunks, AXES, split_axis=0, concat_axis=0, axis_index_grou...  66.7 us
    all_to_all x2, starting transfers between devices, exchange(): lax.all_to_all(chunks, AXES, split_axis=0, concat_axis=0, axis_index_grou...  39.4 us
    ppermute x1, waiting for transfers between devices, summed_grads(): down_other = lax.ppermute(down, 'dp', OTHER_CHIP)  33.1 us
    ppermute x1, starting transfers between devices, expert_weights(): theirs = lax.ppermute(mine, 'dp', OTHER_CORE)  23.7 us
    ppermute x1, waiting for transfers between devices, summed_grads(): gate_up_other = lax.ppermute(gate_up, 'dp', OTHER_CHIP)  12.1 us
    pallas_call x1, Pallas kernels, expert_rows(): pl.pallas_call(functools.partial(expert_kernel, cap), in_specs=[anywhere(...  9.99 us
    pallas_call x2, Pallas kernels, partial_grads(): pl.pallas_call(functools.partial(kernel, cap), grid_spec=pltpu.PrefetchSc...  9.99 us
    unnamed x14, local copies, waits for them, and re-layouts  6.87 us
  transfers between devices with their start and end apart: 8, of which 5 were waited for; matrix products, arithmetic and copies ran while one was open for 0% of the time, Pallas kernels for 6%

profile of v5, /device:TPU:1, one launch (start us, length us, event | category | flops | bytes accessed | tf_op | source)
XLA Modules:
  0.0 240.2 jit_solution(5838849024850172217)
XLA Ops:
  0.6 5.4 %shard_map.111 = (bf16[1024,2048]{1,0:T(8,128)(2,1)}, s32[128,128]{1,0:T(8,128)}, bf16[3,512,384]{2,1,0:T(8,128)(2,1)}) custom-call(s32[2,128]{1,0:T(2,128)} %bitcast.24, f32[2,128]{1,0:T(2,128)} %bitcast.25, f32[16,128]{1,0:T(8,128)} %bitcast.23, bf16[128,2048]{1,0:T(8,128)(2,1)} %codes_ref.1, bf16[128,2048]{1,0:T(8,128)(2,1)} %grad_ref.1, ...), custom_call_target="tpu_custom_call" | custom-call | flops 274877906944 | bytes 6291456 | tf_op jit(solution)/shard_map/pallas_call | solution.py:140
  6.0 4.0 %collective-permute-start = (bf16[3,512,384]{2,1,0:T(8,128)(2,1)}, bf16[3,512,384]{2,1,0:T(8,128)(2,1)S(1)}, u32[]{:S(2)}, u32[]{:S(2)}) collective-permute-start(bf16[3,512,384]{2,1,0:T(8,128)(2,1)} %get-tuple-element.21.own), channel_id=1, source_target_pairs={{0,256},{256,0},{128,384},{384,128},{1,257},{257,1},{129,385},{385... | collective-permute-start | bytes 3538952 | tf_op jit(solution)/shard_map/ppermute | solution.py:172
  10.1 19.7 %all-to-all-start = ((bf16[128,8,2048]{2,1,0:T(8,128)(2,1)}), bf16[128,8,2048]{2,1,0:T(8,128)(2,1)}, u32[]{:S(2)}, u32[]{:S(2)}) async-start(bf16[128,8,2048]{2,1,0:T(8,128)(2,1)} %bitcast.15), calls=%async_computation | async-start | bytes 8388608 | tf_op jit(solution)/shard_map/all_to_all | solution.py:434
  29.7 1.5 collective-permute-done.chip
  32.3 1.3 copy-done.5
  33.8 23.7 %collective-permute-start.1 = (bf16[2,3,512,384]{3,2,1,0:T(8,128)(2,1)S(1)}, bf16[2,3,512,384]{3,2,1,0:T(8,128)(2,1)}, u32[]{:S(2)}, u32[]{:S(2)}) collective-permute-start(bf16[2,3,512,384]{3,2,1,0:T(8,128)(2,1)S(1)} %shard_map.112.mine), channel_id=1, source_target_pairs={{0,128},{128,0},{256,384},{384,256},{1,129},{129,1},{257,385},{385... | collective-permute-start | bytes 7077896 | tf_op jit(solution)/shard_map/ppermute | solution.py:174
  57.5 4.3 %collective-permute-done.1.theirs = bf16[2,3,512,384]{3,2,1,0:T(8,128)(2,1)} collective-permute-done((bf16[2,3,512,384]{3,2,1,0:T(8,128)(2,1)S(1)}, bf16[2,3,512,384]{3,2,1,0:T(8,128)(2,1)}, u32[]{:S(2)}, u32[]{:S(2)}) %collective-permute-start.1) | collective-permute-done | bytes 2359328 | tf_op jit(solution)/shard_map/ppermute | solution.py:174
  61.8 2.1 shard_map.113
  63.9 1.7 copy-done.1
  65.6 1.1 copy-done.2
  66.7 66.7 %all-to-all-done = bf16[128,8,2048]{2,1,0:T(8,128)(2,1)} async-done(((bf16[128,8,2048]{2,1,0:T(8,128)(2,1)}), bf16[128,8,2048]{2,1,0:T(8,128)(2,1)}, u32[]{:S(2)}, u32[]{:S(2)}) %all-to-all-start) | async-done | bytes 4194336 | tf_op jit(solution)/shard_map/all_to_all | solution.py:434
  133.4 10.0 %shard_map.114 = (bf16[1024,1024]{1,0:T(8,128)(2,1)}, bf16[512,768]{1,0:T(8,128)(2,1)}, bf16[512,384]{1,0:T(8,128)(2,1)}) custom-call(bf16[1024,2048]{1,0:T(8,128)(2,1)} %bitcast.7.recv, bf16[2048,768]{1,0:T(8,128)(2,1)} %copy-done.1, bf16[2048,384]{1,0:T(8,128)(2,1)} %copy-done.2), custom_call_target="tpu_custom_call" | custom-call | flops 4026531840 | bytes 16777216 | tf_op jit(solution)/shard_map/pallas_call | solution.py:284
  143.4 19.8 %all-to-all-start.1 = ((bf16[128,8,1024]{2,1,0:T(8,128)(2,1)}), bf16[128,8,1024]{2,1,0:T(8,128)(2,1)S(1)}, u32[]{:S(2)}, u32[]{:S(2)}) async-start(bf16[128,8,1024]{2,1,0:T(8,128)(2,1)} %bitcast.16), calls=%async_computation.1 | async-start | bytes 4194304 | tf_op jit(solution)/shard_map/all_to_all | solution.py:434
  163.2 5.2 %shard_map.116 = (bf16[2,3,384,512]{3,2,1,0:T(8,128)(2,1)}, bf16[1152,512]{1,0:T(8,128)(2,1)}) custom-call(s32[1]{0:T(128)} %bitcast.8.dp_ref, bf16[1024,2048]{1,0:T(8,128)(2,1)} %bitcast.7.recv, bf16[512,768]{1,0:T(8,128)(2,1)} %get-tuple-element.25.d_gu, bf16[512,384]{1,0:T(8,128)(2,1)} %get-tuple-element.26.hidden), custom_call_target="tpu_custom_call" | custom-call | flops 1207959552 | bytes 6291456 | tf_op jit(solution)/shard_map/pallas_call | solution.py:341
  168.4 5.7 %collective-permute-start.2 = (bf16[2,3,384,512]{3,2,1,0:T(8,128)(2,1)}, bf16[2,3,384,512]{3,2,1,0:T(8,128)(2,1)S(1)}, u32[]{:S(2)}, u32[]{:S(2)}) collective-permute-start(bf16[2,3,384,512]{3,2,1,0:T(8,128)(2,1)} %get-tuple-element.28), channel_id=1, source_target_pairs={{0,128},{128,0},{256,384},{384,256},{1,129},{129,1},{257,385},{385... | collective-permute-start | bytes 7077896 | tf_op jit(solution)/shard_map/ppermute | solution.py:389
  174.1 4.7 %shard_map.117.even = bf16[2,3,384,512]{3,2,1,0:T(8,128)(2,1)} custom-call(s32[1]{0:T(128)} %bitcast.8.dp_ref, bf16[1024,2048]{1,0:T(8,128)(2,1)} %bitcast.7.recv, bf16[1152,512]{1,0:T(8,128)(2,1)} %get-tuple-element.27.turned), custom_call_target="tpu_custom_call" | custom-call | flops 1207959552 | bytes 6291456 | tf_op jit(solution)/shard_map/pallas_call | solution.py:341
  178.9 1.7 copy-done
  181.1 1.9 collective-permute-start.4
  183.0 3.4 %collective-permute-start.3 = (bf16[2,384,512]{2,1,0:T(8,128)(2,1)S(1)}, bf16[2,384,512]{2,1,0:T(8,128)(2,1)S(1)}, u32[]{:S(2)}, u32[]{:S(2)}) collective-permute-start(bf16[2,384,512]{2,1,0:T(8,128)(2,1)S(1)} %get-tuple-element.30), channel_id=1, source_target_pairs={{0,256},{256,0},{128,384},{384,128},{1,257},{257,1},{129,385},{385... | collective-permute-start | bytes 2359304 | tf_op jit(solution)/shard_map/ppermute | solution.py:394
  186.4 33.1 %collective-permute-done.4.other = bf16[2,384,512]{2,1,0:T(8,128)(2,1)S(1)} collective-permute-done((bf16[2,384,512]{2,1,0:T(8,128)(2,1)S(1)}, bf16[2,384,512]{2,1,0:T(8,128)(2,1)S(1)}, u32[]{:S(2)}, u32[]{:S(2)}) %collective-permute-start.4) | collective-permute-done | bytes 786464 | tf_op jit(solution)/shard_map/ppermute | solution.py:393
  219.6 4.5 %collective-permute-start.5 = (bf16[2,384,512]{2,1,0:T(8,128)(2,1)S(1)}, bf16[2,384,512]{2,1,0:T(8,128)(2,1)S(1)}, u32[]{:S(2)}, u32[]{:S(2)}) collective-permute-start(bf16[2,384,512]{2,1,0:T(8,128)(2,1)S(1)} %shard_map.120.even), channel_id=1, source_target_pairs={{0,128},{128,0},{256,384},{384,256},{1,129},{129,1},{257,385},{385... | collective-permute-start | bytes 2359304 | tf_op jit(solution)/shard_map/ppermute | solution.py:396
  224.2 12.1 %collective-permute-done.3.other = bf16[2,384,512]{2,1,0:T(8,128)(2,1)S(1)} collective-permute-done((bf16[2,384,512]{2,1,0:T(8,128)(2,1)S(1)}, bf16[2,384,512]{2,1,0:T(8,128)(2,1)S(1)}, u32[]{:S(2)}, u32[]{:S(2)}) %collective-permute-start.3) | collective-permute-done | bytes 786464 | tf_op jit(solution)/shard_map/ppermute | solution.py:394
  237.4 1.3 shard_map.121
  238.6 1.6 shard_map.115
  (17 shorter events, 3.1 us)
Async XLA Ops:
  6.0 25.2 %collective-permute-start = (bf16[3,512,384]{2,1,0:T(8,128)(2,1)}, bf16[3,512,384]{2,1,0:T(8,128)(2,1)S(1)}, u32[]{:S(2)}, u32[]{:S(2)}) collective-permute-start(bf16[3,512,384]{2,1,0:T(8,128)(2,1)} %get-tuple-element.21.own), channel_id=1, source_target_pairs={{0,256},{256,0},{128,384},{384,128},{1,257},{257,1},{129,385},{385... | collective-permute-start | bytes 3538952 | tf_op jit(solution)/shard_map/ppermute | solution.py:172
  10.1 22.3 %copy-start.3 = (bf16[3,512,384]{2,1,0:T(8,128)(2,1)S(1)}, bf16[3,512,384]{2,1,0:T(8,128)(2,1)}, u32[]{:S(2)}) copy-start(bf16[3,512,384]{2,1,0:T(8,128)(2,1)} %get-tuple-element.21.own) | copy-start | bytes 3538948
  10.1 123.4 %all-to-all-start = ((bf16[128,8,2048]{2,1,0:T(8,128)(2,1)}), bf16[128,8,2048]{2,1,0:T(8,128)(2,1)}, u32[]{:S(2)}, u32[]{:S(2)}) async-start(bf16[128,8,2048]{2,1,0:T(8,128)(2,1)} %bitcast.15), calls=%async_computation | async-start | bytes 8388608 | tf_op jit(solution)/shard_map/all_to_all | solution.py:434
  31.2 1.1 copy-start.4
  32.3 1.3 copy-start.5
  33.8 28.0 %collective-permute-start.1 = (bf16[2,3,512,384]{3,2,1,0:T(8,128)(2,1)S(1)}, bf16[2,3,512,384]{3,2,1,0:T(8,128)(2,1)}, u32[]{:S(2)}, u32[]{:S(2)}) collective-permute-start(bf16[2,3,512,384]{3,2,1,0:T(8,128)(2,1)S(1)} %shard_map.112.mine), channel_id=1, source_target_pairs={{0,128},{128,0},{256,384},{384,256},{1,129},{129,1},{257,385},{385... | collective-permute-start | bytes 7077896 | tf_op jit(solution)/shard_map/ppermute | solution.py:174
  63.9 1.7 copy-start.1
  65.6 1.1 copy-start.2
  143.4 95.2 %all-to-all-start.1 = ((bf16[128,8,1024]{2,1,0:T(8,128)(2,1)}), bf16[128,8,1024]{2,1,0:T(8,128)(2,1)S(1)}, u32[]{:S(2)}, u32[]{:S(2)}) async-start(bf16[128,8,1024]{2,1,0:T(8,128)(2,1)} %bitcast.16), calls=%async_computation.1 | async-start | bytes 4194304 | tf_op jit(solution)/shard_map/all_to_all | solution.py:434
  168.4 10.5 %collective-permute-start.2 = (bf16[2,3,384,512]{3,2,1,0:T(8,128)(2,1)}, bf16[2,3,384,512]{3,2,1,0:T(8,128)(2,1)S(1)}, u32[]{:S(2)}, u32[]{:S(2)}) collective-permute-start(bf16[2,3,384,512]{3,2,1,0:T(8,128)(2,1)} %get-tuple-element.28), channel_id=1, source_target_pairs={{0,128},{128,0},{256,384},{384,256},{1,129},{129,1},{257,385},{385... | collective-permute-start | bytes 7077896 | tf_op jit(solution)/shard_map/ppermute | solution.py:389
  178.9 1.7 copy-start
  181.1 38.4 %collective-permute-start.4 = (bf16[2,384,512]{2,1,0:T(8,128)(2,1)S(1)}, bf16[2,384,512]{2,1,0:T(8,128)(2,1)S(1)}, u32[]{:S(2)}, u32[]{:S(2)}) collective-permute-start(bf16[2,384,512]{2,1,0:T(8,128)(2,1)S(1)} %get-tuple-element.33.sent), channel_id=1, source_target_pairs={{0,256},{256,0},{128,384},{384,128},{1,257},{257,1},{129,385},{385... | collective-permute-start | bytes 2359304 | tf_op jit(solution)/shard_map/ppermute | solution.py:393
  183.0 53.3 %collective-permute-start.3 = (bf16[2,384,512]{2,1,0:T(8,128)(2,1)S(1)}, bf16[2,384,512]{2,1,0:T(8,128)(2,1)S(1)}, u32[]{:S(2)}, u32[]{:S(2)}) collective-permute-start(bf16[2,384,512]{2,1,0:T(8,128)(2,1)S(1)} %get-tuple-element.30), channel_id=1, source_target_pairs={{0,256},{256,0},{128,384},{384,128},{1,257},{257,1},{129,385},{385... | collective-permute-start | bytes 2359304 | tf_op jit(solution)/shard_map/ppermute | solution.py:394
  219.6 17.7 %collective-permute-start.5 = (bf16[2,384,512]{2,1,0:T(8,128)(2,1)S(1)}, bf16[2,384,512]{2,1,0:T(8,128)(2,1)S(1)}, u32[]{:S(2)}, u32[]{:S(2)}) collective-permute-start(bf16[2,384,512]{2,1,0:T(8,128)(2,1)S(1)} %shard_map.120.even), channel_id=1, source_target_pairs={{0,128},{128,0},{256,384},{384,256},{1,129},{129,1},{257,385},{385... | collective-permute-start | bytes 2359304 | tf_op jit(solution)/shard_map/ppermute | solution.py:396
  236.3 2.3 copy-start.6
